TPU v7x, 256 devices: a whole 4x4x8 slice. The times are simulated.
256 devices in a mesh: dp: 16 (over z, core), proto: 16 (over x, y).
Axes of the slice: x: 4, y: 4, z: 8, core: 2. Of those that a mesh axis runs over, the one named last changes fastest.
Arguments:
- student_rows: bfloat16 [64, 256, 256], P('dp'), may hold values from -8 to 8
- teacher_rows: bfloat16 [64, 256, 256], P('dp'), may hold values from -8 to 8
- prototypes: bfloat16 [256, 131072], P(None, 'proto'), may hold values from -8 to 8
- center: float32 [131072], P('proto'), may hold values from -1.2 to 1.2
- mask_index: int32 [64, 128], P('dp'), may hold values from 0 to 255, as said below
- mask_count: int32 [64], P('dp'), may hold values from 0 to 128, as said below
- loss_scale: float32 [], replicated, may hold values from 1024 to 4096
Outputs:
- loss: float32 [], replicated
- student_grad: float32 [64, 256, 256], P('dp')
- proto_grad: float32 [131072, 256], P(('proto', 'dp'))
- patch_center: float32 [131072], P('proto')
Inputs may be any that keep to these rules, and one draw needn't show every extreme that they name: `mask_index`: for each image the first mask_count entries are distinct patch numbers; the later entries are patch numbers that are ignored. `mask_count`: the counts of all 64 images sum to 4096; some images have no masked patch.
All inputs are finite; a program needn't handle non-finite values.
Results may differ from a plain program's by a relative error of at most 0.022.
Values may be sent and summed in bfloat16 or wider, within the bound.
No kernel may reach another device: no remote copies, remote signals or barrier semaphores. Data moves between devices by JAX's collectives and lax.ppermute only.
A program may use at most 128 MiB of HBM per device.

v0:
```python
import functools
import math

import jax
import jax.numpy as jnp
from jax import lax
from jax.experimental import pallas as pl
from jax.experimental.pallas import tpu as pltpu
from jax.sharding import Mesh, PartitionSpec as P

bf16 = jnp.bfloat16
f32 = jnp.float32
log2e = math.log2(math.e)
ln2 = math.log(2.0)
t_scale = log2e / 0.04
s_scale = log2e / 0.1
inverse_temp = 10.0
norm_epsilon = 1e-06
low = -1e30

Z, CORES, X, Y = 8, 2, 4, 4
D = 256
SLOTS = 128
IMAGES = 64
TOTAL = 4096
LOCAL = 4
ROWS = LOCAL * SLOTS
BOTH = 2 * ROWS
CHUNK = 512
TILE = 512
STAT_TILE = 256
EXTRA = 48
HELD = ROWS + 16
STATS = 5
PEERS = CORES * X * Y
OFFSETS = (4, -3, 3, -2, 2, -1, 1, 0)
PIECES = 4

NT = (((1,), (1,)), ((), ()))
TN = (((0,), (0,)), ((), ()))


def dot(a, b, dims=(((1,), (0,)), ((), ()))):
    return lax.dot_general(a, b, dims, preferred_element_type=f32)


def params(mebibytes=16):
    return pltpu.CompilerParams(vmem_limit_bytes=mebibytes * 1024 * 1024)


def cost(flops, nbytes, trans=0):
    return pl.CostEstimate(flops=flops, bytes_accessed=nbytes, transcendentals=trans)


def picks(index_ref, count, i):
    patch = lax.broadcasted_iota(jnp.int32, (D, SLOTS), 0)
    slot = lax.broadcasted_iota(jnp.int32, (D, SLOTS), 1)
    hit = (patch == index_ref[i : i + 1, :]) & (slot < count)
    return jnp.where(hit, 1.0, 0.0).astype(bf16)


def unit_rows(values):
    length = jnp.sqrt(jnp.sum(values * values, axis=1, keepdims=True) + norm_epsilon)
    return values / length, length


def prep_kernel(count_ref, index_ref, s_ref, t_ref, out_ref):
    for i in range(LOCAL):
        pick = picks(index_ref, count_ref[i], i)
        for which, ref in enumerate((s_ref, t_ref)):
            unit, _ = unit_rows(dot(pick, ref[i], TN))
            out_ref[which, i * SLOTS : (i + 1) * SLOTS, :] = unit.astype(bf16)
    row = lax.broadcasted_iota(jnp.int32, (HELD - ROWS, D), 0)
    counts = jnp.zeros((HELD - ROWS, D), jnp.int32)
    for i in range(LOCAL):
        counts = jnp.where(row == i, count_ref[i], counts)
    for which in range(2):
        out_ref[which, ROWS:, :] = counts.astype(f32).astype(bf16)


def prep(count, index, student, teacher):
    smem = pl.BlockSpec(memory_space=pltpu.SMEM)
    vmem = pl.BlockSpec(memory_space=pltpu.VMEM)
    return pl.pallas_call(
        prep_kernel,
        out_shape=jax.ShapeDtypeStruct((2, HELD, D), bf16),
        in_specs=[smem, vmem, vmem, vmem],
        out_specs=vmem,
        compiler_params=params(),
        cost_estimate=cost(2 * 2 * ROWS * D * D, 1 << 21),
    )(count, index, student, teacher)


def wide(block, times):
    return jnp.concatenate([block] * times, axis=1)


def chunk_columns(i, core):
    return pl.ds(pl.multiple_of((CORES * i + core) * CHUNK, CHUNK), CHUNK)


def turned(held):
    return jnp.broadcast_to(held * -t_scale, (128, CHUNK)).T


def stats_kernel(ids_ref, p_ref, c_ref, mine_ref, other_ref, block, sum_ref, acc):
    groups = (CHUNK // 8, 8, STAT_TILE)
    for i in range(Z):
        columns = chunk_columns(i, ids_ref[1])
        protos = p_ref[:, columns].T
        shift = wide(turned(c_ref[:, columns]), STAT_TILE // 128)
        for half, ref in enumerate((mine_ref, other_ref)):
            for j in range(ROWS // STAT_TILE):
                rows = slice(j * STAT_TILE, (j + 1) * STAT_TILE)
                at = slice(half * ROWS + j * STAT_TILE, half * ROWS + (j + 1) * STAT_TILE)
                t_arg = (dot(protos, ref[1, rows, :], NT) * t_scale + shift).reshape(groups)
                s_arg = (dot(protos, ref[0, rows, :], NT) * s_scale).reshape(groups)
                t_top = jnp.max(t_arg, axis=0)
                s_top = jnp.max(s_arg, axis=0)
                t_exp = jnp.exp2(t_arg - t_top[None])
                s_exp = jnp.exp2(s_arg - s_top[None])
                acc[0, i, :, at] = t_top
                acc[1, i, :, at] = jnp.sum(t_exp, axis=0)
                acc[2, i, :, at] = jnp.sum(t_exp * s_arg, axis=0)
                acc[3, i, :, at] = s_top
                acc[4, i, :, at] = jnp.sum(s_exp, axis=0)
    for g in range(BOTH // 128):
        at = slice(g * 128, (g + 1) * 128)
        parts = [acc[q, :, :, at].reshape(Z * 8, 128) for q in range(STATS)]
        t_top = jnp.max(parts[0], axis=0, keepdims=True)
        s_top = jnp.max(parts[3], axis=0, keepdims=True)
        t_keep = jnp.exp2(parts[0] - t_top)
        s_keep = jnp.exp2(parts[3] - s_top)
        merged_rows = (
            t_top,
            jnp.sum(parts[1] * t_keep, axis=0, keepdims=True),
            jnp.sum(parts[2] * t_keep, axis=0, keepdims=True),
            s_top,
            jnp.sum(parts[4] * s_keep, axis=0, keepdims=True),
        )
        for q in range(STATS):
            block[q * 8 + g : q * 8 + g + 1, :] = merged_rows[q]
    first = jnp.sum(mine_ref[1, :ROWS, :].astype(f32), axis=0, keepdims=True)
    second = jnp.sum(other_ref[1, :ROWS, :].astype(f32), axis=0, keepdims=True)
    sum_ref[...] = jnp.broadcast_to(first + second, (8, D))


def local_stats(ids, prototypes, center, mine, other):
    smem = pl.BlockSpec(memory_space=pltpu.SMEM)
    vmem = pl.BlockSpec(memory_space=pltpu.VMEM)
    return pl.pallas_call(
        stats_kernel,
        in_specs=[smem, vmem, vmem, vmem, vmem],
        out_specs=[vmem] * 2,
        out_shape=[jax.ShapeDtypeStruct((STATS * 8, 128), f32), jax.ShapeDtypeStruct((8, D), f32)],
        scratch_shapes=[pltpu.VMEM((STATS, Z, 8, BOTH), f32)],
        compiler_params=params(24),
        cost_estimate=cost(4 * BOTH * Z * CHUNK * D, 6 << 20, 2 * BOTH * Z * CHUNK),
    )(ids, prototypes, center, mine, other)


def split3(value):
    top = value.astype(bf16)
    rest = value - top.astype(f32)
    middle = rest.astype(bf16)
    return top, middle, (rest - middle.astype(f32)).astype(bf16)


def tree(parts):
    while len(parts) > 1:
        parts = [parts[i] + parts[i + 1] for i in range(0, len(parts), 2)]
    return parts[0]


def merge(parts):
    t_top = functools.reduce(jnp.maximum, [p[0] for p in parts])
    s_top = functools.reduce(jnp.maximum, [p[3] for p in parts])
    t_keep = [jnp.exp2(p[0] - t_top) for p in parts]
    s_keep = [jnp.exp2(p[3] - s_top) for p in parts]
    t_sum = tree([p[1] * k for p, k in zip(parts, t_keep)])
    cross = tree([p[2] * k for p, k in zip(parts, t_keep)])
    s_sum = tree([p[4] * k for p, k in zip(parts, s_keep)])
    return t_top, t_sum, cross, s_top, s_sum


def flip(value):
    return jnp.concatenate([value[LOCAL:], value[:LOCAL]], axis=0)


def rows_of(ref):
    return [ref[q * 8 : (q + 1) * 8, :] for q in range(STATS)]


def core_merge_kernel(mine_ref, got_ref, out_ref):
    parts = [rows_of(mine_ref), [flip(value) for value in rows_of(got_ref)]]
    for q, value in enumerate(merge(parts)):
        out_ref[q * 8 : (q + 1) * 8, :] = value


def y_merge_kernel(a, b, c, d, out_ref):
    for q, value in enumerate(merge([rows_of(ref) for ref in (a, b, c, d)])):
        out_ref[q * 8 : (q + 1) * 8, :] = value


def x_merge_kernel(ids_ref, scale_ref, a, b, c, d, mine_ref, other_ref, sum_ref, coef_ref, misc_ref):
    t_top, t_sum, cross, s_top, s_sum = merge([rows_of(ref) for ref in (a, b, c, d)])
    counts = [ref[0, ROWS:, :128].astype(f32)[:LOCAL] for ref in (mine_ref, other_ref)]
    count = jnp.concatenate(counts, axis=0)
    slot = lax.broadcasted_iota(jnp.int32, (8, 128), 1).astype(f32)
    live = slot < count
    weight = 1.0 / (IMAGES * jnp.maximum(count, 1.0))
    s_lse = s_top + jnp.log2(s_sum)
    ce = (s_lse - cross / t_sum) * ln2
    factor = jnp.log2(weight * (scale_ref[0] * inverse_temp))
    s_coef = jnp.where(live, factor - s_lse, low)
    t_coef = jnp.where(live, factor - t_top - jnp.log2(t_sum), low)
    for g in range(8):
        coef_ref[0:1, g * 128 : (g + 1) * 128] = s_coef[g : g + 1]
        coef_ref[1:2, g * 128 : (g + 1) * 128] = t_coef[g : g + 1]
    coef_ref[2:8, :] = jnp.zeros((6, BOTH), f32)
    part = jnp.sum(jnp.where(live, weight * ce, 0.0), axis=1, keepdims=True)
    first = jnp.sum(part[:LOCAL], axis=0, keepdims=True)
    second = jnp.sum(part[LOCAL:], axis=0, keepdims=True)
    row = lax.broadcasted_iota(jnp.int32, (EXTRA, D), 0)
    mine = jnp.bitwise_and(row, Z - 1) == ids_ref[0]
    row_sum = split3(sum_ref[0:1, :])
    losses = split3(jnp.broadcast_to(first + second, (1, D)))
    block = jnp.zeros((EXTRA, D), f32)
    for i in range(3):
        block = jnp.where(row // Z == i, row_sum[i].astype(f32), block)
        block = jnp.where(row // Z == 3 + i, losses[i].astype(f32), block)
    misc_ref[...] = jnp.where(mine, block, 0.0).astype(bf16)


def small_call(kernel, out_shape, *args, smem=()):
    specs = [
        pl.BlockSpec(memory_space=pltpu.SMEM if i in smem else pltpu.VMEM) for i in range(len(args))
    ]
    vmem = pl.BlockSpec(memory_space=pltpu.VMEM)
    return pl.pallas_call(
        kernel,
        out_shape=out_shape,
        in_specs=specs,
        out_specs=jax.tree.map(lambda _: vmem, out_shape),
        compiler_params=params(),
        cost_estimate=cost(1 << 20, 1 << 18),
    )(*args)


def grad_kernel(ids_ref, p_ref, c_ref, mine_ref, other_ref, coef_ref, misc_ref, *refs):
    n = len(OFFSETS)
    outs, send_ref, du_ref = refs[: n + 1], refs[n + 1], refs[n + 2]
    core = ids_ref[1]
    order = [lax.rem(ids_ref[0] + Z + d * (1 - 2 * core), Z) for d in OFFSETS]
    for i in range(n):
        columns = chunk_columns(order[i], core)
        wide_p = p_ref[:, columns]
        protos = wide_p.T
        shift = wide(turned(c_ref[:, columns]), TILE // 128)
        total = None
        for half, ref in enumerate((mine_ref, other_ref)):
            for j in range(ROWS // TILE):
                rows = slice(j * TILE, (j + 1) * TILE)
                at = slice(half * ROWS + j * TILE, half * ROWS + (j + 1) * TILE)
                s_rows = ref[0, rows, :]
                t_arg = dot(protos, ref[1, rows, :], NT) * t_scale + shift + coef_ref[1:2, at]
                s_arg = dot(protos, s_rows, NT) * s_scale + coef_ref[0:1, at]
                dlogit = (jnp.exp2(s_arg) - jnp.exp2(t_arg)).astype(bf16)
                part = dot(dlogit, s_rows)
                total = part if total is None else total + part
                du = dot(wide_p, dlogit)
                if i == 0:
                    du_ref[:, at] = du
                else:
                    du_ref[:, at] += du
        if i == 0:
            half = CHUNK // 2
            outs[0][:half, :] = total[:half].astype(bf16)
            outs[0][half:, :] = misc_ref[...]
            outs[1][...] = total[half:].astype(bf16)
        else:
            outs[i + 1][...] = total.astype(bf16)
    send_ref[core] = du_ref[:, :ROWS].astype(bf16)
    send_ref[1 - core] = du_ref[:, ROWS:].astype(bf16)


def grads(ids, prototypes, center, mine, other, coef, misc):
    smem = pl.BlockSpec(memory_space=pltpu.SMEM)
    vmem = pl.BlockSpec(memory_space=pltpu.VMEM)
    n = len(OFFSETS)
    shapes = [(CHUNK // 2 + EXTRA, D), (CHUNK // 2, D)] + [(CHUNK, D)] * (n - 1) + [(CORES, D, ROWS)]
    return pl.pallas_call(
        grad_kernel,
        in_specs=[smem] + [vmem] * 6,
        out_specs=[vmem] * len(shapes),
        out_shape=[jax.ShapeDtypeStruct(shape, bf16) for shape in shapes],
        scratch_shapes=[pltpu.VMEM((D, BOTH), f32)],
        compiler_params=params(24),
        cost_estimate=cost(8 * BOTH * n * CHUNK * D, n << 20, 2 * BOTH * n * CHUNK),
    )(ids, prototypes, center, mine, other, coef, misc)


def du_sum_kernel(got_ref, out_ref):
    total = jnp.sum(got_ref[...].astype(f32), axis=0).astype(bf16)
    out_ref[...] = jnp.broadcast_to(total[None], (X * Y,) + total.shape)


def halves_kernel(offset, with_extra, far_ref, got_ref, misc_ref, out_ref):
    half = CHUNK // 2
    for i in range(2):
        rows = slice(i * half, (i + 1) * half)
        part = far_ref[rows, :].astype(f32)
        if i == offset:
            part = part + got_ref[:half, :].astype(f32)
        out_ref[rows, :] = part.astype(bf16)
    extra = misc_ref[...]
    if with_extra:
        extra = extra + got_ref[half:, :]
    out_ref[CHUNK:, :] = extra


def step_kernel(near_ref, got_ref, misc_ref, out_ref):
    out_ref[:CHUNK, :] = (near_ref[...].astype(f32) + got_ref[:CHUNK, :].astype(f32)).astype(bf16)
    out_ref[CHUNK:, :] = misc_ref[...] + got_ref[CHUNK:, :]


def finish_kernel(near_ref, a_ref, b_ref, misc_ref, p_ref, grad_ref, center_ref, loss_ref):
    width = p_ref.shape[1] // PIECES
    pieces = [pl.ds(i * width, width) for i in range(PIECES)]
    total = near_ref[...].astype(f32) + a_ref[:CHUNK, :].astype(f32)
    grad_ref[...] = total + b_ref[:CHUNK, :].astype(f32)
    extra = (misc_ref[...] + a_ref[CHUNK:, :] + b_ref[CHUNK:, :]).astype(f32)
    first = extra[0:8] + extra[8:16] + extra[16:24]
    loss = extra[24:32] + extra[32:40] + extra[40:48]
    total = jnp.broadcast_to(jnp.sum(first, axis=0, keepdims=True), (16, D))
    loss_ref[0, 0] = jnp.sum(loss[:, 0:1])
    stacked = jnp.concatenate(split3(total), axis=0)
    for at in pieces:
        three = dot(stacked, p_ref[:, at])
        center_ref[:, at] = (three[0:1] + three[16:17] + three[32:33]) * (1.0 / TOTAL)


def finish(near, a, b, misc, prototypes):
    width = prototypes.shape[1]
    smem = pl.BlockSpec(memory_space=pltpu.SMEM)
    vmem = pl.BlockSpec(memory_space=pltpu.VMEM)
    return pl.pallas_call(
        finish_kernel,
        in_specs=[vmem] * 5,
        out_specs=[vmem, vmem, smem],
        out_shape=[
            jax.ShapeDtypeStruct((CHUNK, D), f32),
            jax.ShapeDtypeStruct((1, width), f32),
            jax.ShapeDtypeStruct((1, 1), f32),
        ],
        compiler_params=params(),
        cost_estimate=cost(6 * 8 * D * width, 5 << 20),
    )(near, a, b, misc, prototypes)


def final_kernel(count_ref, index_ref, s_ref, du_ref, out_ref):
    for i in range(LOCAL):
        pick = picks(index_ref, count_ref[i], i)
        unit, length = unit_rows(dot(pick, s_ref[i], TN))
        d_unit = du_ref[:, i * SLOTS : (i + 1) * SLOTS].astype(f32).T
        row = (d_unit - unit * jnp.sum(unit * d_unit, axis=1, keepdims=True)) / length
        top = row.astype(bf16)
        rest = (row - top.astype(f32)).astype(bf16)
        out_ref[i] = dot(pick, top) + dot(pick, rest)


def shards(student_rows, teacher_rows, prototypes, center, mask_index, mask_count, loss_scale):
    z, core, x, y = (lax.axis_index(a) for a in ("z", "core", "x", "y"))
    ids = jnp.stack([z, core, x, y]).astype(jnp.int32)
    peers = ("core", "x", "y")
    one_way, other_way = [], []
    for i in range(Z):
        below, above, here = (i - 1) % Z * CORES, (i + 1) % Z * CORES, i * CORES
        one_way += [(here, below), (here + 1, above + 1)]
        other_way += [(here, above), (here + 1, below + 1)]

    def swaps(value, axis):
        return [lax.ppermute(value, axis, [(i, i ^ k) for i in range(4)]) for k in (1, 2, 3)]

    def ring(value, pairs):
        return lax.ppermute(value, ("z", "core"), pairs)

    mine = prep(mask_count, mask_index, student_rows, teacher_rows)
    other = lax.ppermute(mine, "core", [(0, 1), (1, 0)])
    center = center.reshape(1, -1)
    stats, row_sum = local_stats(ids, prototypes, center, mine, other)
    shape = jax.ShapeDtypeStruct((STATS * 8, 128), f32)
    stats = small_call(core_merge_kernel, shape, stats, lax.ppermute(stats, "core", [(0, 1), (1, 0)]))
    stats = small_call(y_merge_kernel, shape, stats, *swaps(stats, "y"))
    coef, misc = small_call(
        x_merge_kernel,
        [jax.ShapeDtypeStruct((8, BOTH), f32), jax.ShapeDtypeStruct((EXTRA, D), bf16)],
        ids, loss_scale.reshape(1), stats, *swaps(stats, "x"), mine, other, row_sum,
        smem=(0, 1),
    )

    step_shape = jax.ShapeDtypeStruct((CHUNK + EXTRA, D), bf16)
    half_a, half_b, *near, send = grads(ids, prototypes, center, mine, other, coef, misc)
    got_a, got_b = ring(half_a, one_way), ring(half_b, other_way)
    part = D // (X * Y)
    got = lax.all_to_all(send.reshape(PEERS, part, ROWS), peers, 0, 0)
    own = small_call(du_sum_kernel, jax.ShapeDtypeStruct((X * Y, part, ROWS), bf16), got)
    for i in range(3):
        if i == 0:
            kernel_a = functools.partial(halves_kernel, 0, True)
            kernel_b = functools.partial(halves_kernel, 1, False)
        else:
            kernel_a = kernel_b = step_kernel
        send_a = small_call(kernel_a, step_shape, near[2 * i], got_a, misc)
        send_b = small_call(kernel_b, step_shape, near[2 * i + 1], got_b, misc)
        if i == 0:
            send_a, send_b, own = lax.optimization_barrier((send_a, send_b, own))
            du = lax.all_to_all(own, ("x", "y"), 0, 0)
        if i == 2:
            send_a, send_b, du = lax.optimization_barrier((send_a, send_b, du))
        got_a, got_b = ring(send_a, one_way), ring(send_b, other_way)
    proto_grad, patch_center, loss = finish(near[6], got_a, got_b, misc, prototypes)
    student_grad = small_call(
        final_kernel,
        jax.ShapeDtypeStruct(student_rows.shape, f32),
        mask_count, mask_index, student_rows, du.reshape(D, ROWS),
        smem=(0,),
    )
    return (loss.reshape(()), student_grad, proto_grad, patch_center.reshape(-1))


def solution(mesh):
    fine = Mesh(mesh.devices.reshape(Z, CORES, X, Y), ("z", "core", "x", "y"))
    dp, proto = ("z", "core"), ("x", "y")
    in_specs = (
        P(dp, None, None),
        P(dp, None, None),
        P(None, proto),
        P(proto),
        P(dp, None),
        P(dp),
        P(),
    )
    out_specs = (P(), P(dp, None, None), P(proto + dp, None), P(proto))
    return jax.shard_map(shards, mesh=fine, in_specs=in_specs, out_specs=out_specs, check_vma=False)
```

profile of v0, /device:TPU:8, one launch (start us, length us, event | category | flops | bytes accessed | tf_op | source)
XLA Modules:
  0.0 114.6 jit_solution(3379365290784304176)
XLA Ops:
  0.6 0.0 copy-start.3
  0.6 1.0 copy-done.3
  1.7 1.0 copy-done.5
  2.7 0.7 copy-done.6
  3.4 0.7 copy-done.8
  4.1 1.1 shard_map.102.mine_ref
  5.1 0.1 collective-permute-start
  5.2 0.1 pad_add_fusion.ids_ref
  5.3 1.8 %collective-permute-done.other_ref = bf16[2,528,256]{2,1,0:T(8,128)(2,1)S(1)} collective-permute-done((bf16[2,528,256]{2,1,0:T(8,128)(2,1)S(1)}, bf16[2,528,256]{2,1,0:T(8,128)(2,1)S(1)}, u32[]{:S(2)}, u32[]{:S(2)}) %collective-permute-start) | collective-permute-done | bytes 540704 | tf_op jit(solution)/shard_map/ppermute | solution.py:389
  7.2 2.2 %copy-done = bf16[256,8192]{1,0:T(8,128)(2,1)S(1)} copy-done((bf16[256,8192]{1,0:T(8,128)(2,1)S(1)}, bf16[256,8192]{1,0:T(8,128)(2,1)}, u32[]{:S(2)}) %copy-start) | copy-done | bytes 4194328
  9.4 0.8 copy-done.12
  10.1 11.4 %shard_map.103 = (f32[40,128]{1,0:T(8,128)S(1)}, f32[8,256]{1,0:T(8,128)S(1)}) custom-call(s32[4]{0:T(128)S(1)} %pad_add_fusion.ids_ref, bf16[256,8192]{1,0:T(8,128)(2,1)S(1)} %copy-done, f32[1,8192]{1,0:T(1,128)S(1)} %bitcast.12, bf16[2,528,256]{2,1,0:T(8,128)(2,1)S(1)} %shard_map.102.mine_ref, bf16[2,528,256]{2,1,0:T(8,128)(2,1)S(1)} %collective-permute-done.other_ref), custom_call_target="tpu_custom_call" | custom-call | flops 4294967296 | bytes 6291456 | tf_op jit(solution)/shard_map/pallas_call | solution.py:151
  21.5 0.4 collective-permute-start.1
  21.9 1.0 collective-permute-done.1.got_ref
  23.0 1.7 %collective-permute-start.4 = (f32[40,128]{1,0:T(8,128)S(1)}, f32[40,128]{1,0:T(8,128)S(1)}, u32[]{:S(2)}, u32[]{:S(2)}) collective-permute-start(f32[40,128]{1,0:T(8,128)S(1)} %shard_map.104.a), channel_id=1, source_target_pairs={{0,3},{1,2},{2,1},{3,0},{4,7},{5,6},{6,5},{7,4},{8,11},{9,10},{10,... | collective-permute-start | bytes 61448 | tf_op jit(solution)/shard_map/ppermute | solution.py:383
  24.6 2.7 %collective-permute-start.3 = (f32[40,128]{1,0:T(8,128)S(1)}, f32[40,128]{1,0:T(8,128)S(1)}, u32[]{:S(2)}, u32[]{:S(2)}) collective-permute-start(f32[40,128]{1,0:T(8,128)S(1)} %shard_map.104.a), channel_id=1, source_target_pairs={{0,2},{1,3},{2,0},{3,1},{4,6},{5,7},{6,4},{7,5},{8,10},{9,11},{10,... | collective-permute-start | bytes 61448 | tf_op jit(solution)/shard_map/ppermute | solution.py:383
  27.3 0.0 collective-permute-start.2
  27.3 0.0 collective-permute-done.4.d
  27.3 2.7 %collective-permute-done.3.c = f32[40,128]{1,0:T(8,128)S(1)} collective-permute-done((f32[40,128]{1,0:T(8,128)S(1)}, f32[40,128]{1,0:T(8,128)S(1)}, u32[]{:S(2)}, u32[]{:S(2)}) %collective-permute-start.3) | collective-permute-done | bytes 20512 | tf_op jit(solution)/shard_map/ppermute | solution.py:383
  30.0 1.0 collective-permute-done.2.b
  31.1 1.8 %collective-permute-start.7 = (f32[40,128]{1,0:T(8,128)S(1)}, f32[40,128]{1,0:T(8,128)S(1)}, u32[]{:S(2)}, u32[]{:S(2)}) collective-permute-start(f32[40,128]{1,0:T(8,128)S(1)} %shard_map.105.a), channel_id=1, source_target_pairs={{0,12},{4,8},{8,4},{12,0},{1,13},{5,9},{9,5},{13,1},{2,14},{6,10},... | collective-permute-start | bytes 61448 | tf_op jit(solution)/shard_map/ppermute | solution.py:383
  32.9 0.8 collective-permute-start.6
  33.7 1.6 %collective-permute-start.5 = (f32[40,128]{1,0:T(8,128)S(1)}, f32[40,128]{1,0:T(8,128)S(1)}, u32[]{:S(2)}, u32[]{:S(2)}) collective-permute-start(f32[40,128]{1,0:T(8,128)S(1)} %shard_map.105.a), channel_id=1, source_target_pairs={{0,4},{4,0},{8,12},{12,8},{1,5},{5,1},{9,13},{13,9},{2,6},{6,2},{1... | collective-permute-start | bytes 61448 | tf_op jit(solution)/shard_map/ppermute | solution.py:383
  35.9 0.2 collective-permute-done.7.d
  36.2 2.0 %collective-permute-done.6.c = f32[40,128]{1,0:T(8,128)S(1)} collective-permute-done((f32[40,128]{1,0:T(8,128)S(1)}, f32[40,128]{1,0:T(8,128)S(1)}, u32[]{:S(2)}, u32[]{:S(2)}) %collective-permute-start.6) | collective-permute-done | bytes 20512 | tf_op jit(solution)/shard_map/ppermute | solution.py:383
  38.2 0.0 collective-permute-done.5.b
  38.2 0.7 shard_map.106
  38.9 0.0 copy-done.13
  38.9 0.0 copy-start.1
  38.9 2.2 %copy-done.1 = bf16[256,8192]{1,0:T(8,128)(2,1)S(1)} copy-done((bf16[256,8192]{1,0:T(8,128)(2,1)S(1)}, bf16[256,8192]{1,0:T(8,128)(2,1)}, u32[]{:S(2)}) %copy-start.1) | copy-done | bytes 4194328
  41.1 11.1 %shard_map.107 = (bf16[304,256]{1,0:T(8,128)(2,1)S(1)}, bf16[256,256]{1,0:T(8,128)(2,1)S(1)}, bf16[512,256]{1,0:T(8,128)(2,1)S(1)}, bf16[512,256]{1,0:T(8,128)(2...) custom-call(s32[4]{0:T(128)S(1)} %pad_add_fusion.ids_ref, ...), custom_call_target="tpu_custom_call" | custom-call | flops 8589934592 | bytes 8388608 | tf_op jit(solution)/shard_map/pallas_call | solution.py:292
  52.1 0.7 copy-done.10
  52.8 0.6 copy-done.11
  53.4 6.8 %all-to-all-start = ((bf16[32,16,512]{2,1,0:T(8,128)(2,1)}), bf16[32,16,512]{2,1,0:T(8,128)(2,1)S(1)}, u32[]{:S(2)}, u32[]{:S(2)}) async-start(bf16[32,16,512]{2,1,0:T(8,128)(2,1)} %bitcast.6), calls=%async_computation | async-start | bytes 1048576 | tf_op jit(solution)/shard_map/all_to_all | solution.py:406
  60.2 5.9 %collective-permute-start.8 = (bf16[304,256]{1,0:T(8,128)(2,1)}, bf16[304,256]{1,0:T(8,128)(2,1)S(1)}, u32[]{:S(2)}, u32[]{:S(2)}) collective-permute-start(bf16[304,256]{1,0:T(8,128)(2,1)} %copy-done.10), channel_id=1, source_target_pairs={{0,224},{16,48},{32,0},{48,80},{64,32},{80,112},{96,64},{112,144},... | collective-permute-start | bytes 466952 | tf_op jit(solution)/shard_map/ppermute | solution.py:386
  66.2 0.0 collective-permute-start.9
  66.2 6.4 %collective-permute-done.9.got_ref = bf16[256,256]{1,0:T(8,128)(2,1)S(1)} collective-permute-done((bf16[256,256]{1,0:T(8,128)(2,1)}, bf16[256,256]{1,0:T(8,128)(2,1)S(1)}, u32[]{:S(2)}, u32[]{:S(2)}) %collective-permute-start.9) | collective-permute-done | bytes 131104 | tf_op jit(solution)/shard_map/ppermute | solution.py:386
  72.6 0.0 collective-permute-done.8.got_ref
  72.7 0.0 all-to-all-done.got_ref
  72.7 0.8 shard_map.110
  73.5 3.8 %collective-permute-start.10 = (bf16[560,256]{1,0:T(8,128)(2,1)S(1)}, bf16[560,256]{1,0:T(8,128)(2,1)S(1)}, u32[]{:S(2)}, u32[]{:S(2)}) collective-permute-start(bf16[560,256]{1,0:T(8,128)(2,1)S(1)} %shard_map.108), channel_id=1, source_target_pairs={{0,224},{16,48},{32,0},{48,80},{64,32},{80,112},{96,64},{112,144},... | collective-permute-start | bytes 860168 | tf_op jit(solution)/shard_map/ppermute | solution.py:386
  77.3 0.0 collective-permute-start.12
  77.3 6.3 %collective-permute-done.10.got_ref = bf16[560,256]{1,0:T(8,128)(2,1)S(1)} collective-permute-done((bf16[560,256]{1,0:T(8,128)(2,1)S(1)}, bf16[560,256]{1,0:T(8,128)(2,1)S(1)}, u32[]{:S(2)}, u32[]{:S(2)}) %collective-permute-start.10) | collective-permute-done | bytes 286752 | tf_op jit(solution)/shard_map/ppermute | solution.py:386
  83.6 0.1 shard_map.111
  83.7 3.8 %collective-permute-start.11 = (bf16[560,256]{1,0:T(8,128)(2,1)S(1)}, bf16[560,256]{1,0:T(8,128)(2,1)S(1)}, u32[]{:S(2)}, u32[]{:S(2)}) collective-permute-start(bf16[560,256]{1,0:T(8,128)(2,1)S(1)} %shard_map.111), channel_id=1, source_target_pairs={{0,224},{16,48},{32,0},{48,80},{64,32},{80,112},{96,64},{112,144},... | collective-permute-start | bytes 860168 | tf_op jit(solution)/shard_map/ppermute | solution.py:386
  87.4 0.0 collective-permute-done.12.got_ref
  87.4 0.1 shard_map.113
  87.5 0.1 collective-permute-start.13
  87.6 4.9 %all-to-all-start.1 = ((bf16[16,16,512]{2,1,0:T(8,128)(2,1)}), bf16[16,16,512]{2,1,0:T(8,128)(2,1)S(1)}, u32[]{:S(2)}, u32[]{:S(2)}) async-start(bf16[16,16,512]{2,1,0:T(8,128)(2,1)} %shard_map.110), calls=%async_computation.1 | async-start | bytes 524288 | tf_op jit(solution)/shard_map/all_to_all | solution.py:418
  92.5 0.4 collective-permute-done.11.got_ref
  92.9 0.1 shard_map.112
  93.0 2.5 %collective-permute-done.13.got_ref = bf16[560,256]{1,0:T(8,128)(2,1)S(1)} collective-permute-done((bf16[560,256]{1,0:T(8,128)(2,1)S(1)}, bf16[560,256]{1,0:T(8,128)(2,1)S(1)}, u32[]{:S(2)}, u32[]{:S(2)}) %collective-permute-start.13) | collective-permute-done | bytes 286752 | tf_op jit(solution)/shard_map/ppermute | solution.py:386
  95.4 0.1 shard_map.114
  95.5 4.0 %all-to-all-done.1 = bf16[16,16,512]{2,1,0:T(8,128)(2,1)S(1)} async-done(((bf16[16,16,512]{2,1,0:T(8,128)(2,1)}), bf16[16,16,512]{2,1,0:T(8,128)(2,1)S(1)}, u32[]{:S(2)}, u32[]{:S(2)}) %all-to-all-start.1) | async-done | bytes 262176 | tf_op jit(solution)/shard_map/all_to_all | solution.py:418
  99.5 3.2 %collective-permute-start.14 = (bf16[560,256]{1,0:T(8,128)(2,1)S(1)}, bf16[560,256]{1,0:T(8,128)(2,1)S(1)}, u32[]{:S(2)}, u32[]{:S(2)}) collective-permute-start(bf16[560,256]{1,0:T(8,128)(2,1)S(1)} %shard_map.112), channel_id=1, source_target_pairs={{0,224},{16,48},{32,0},{48,80},{64,32},{80,112},{96,64},{112,144},... | collective-permute-start | bytes 860168 | tf_op jit(solution)/shard_map/ppermute | solution.py:386
  102.7 0.0 collective-permute-start.15
  102.7 0.0 copy-done.4
  102.7 0.7 copy-done.7
  103.4 0.7 copy-done.9
  104.1 2.9 %shard_map.116 = f32[4,256,256]{2,1,0:T(8,128)} custom-call(s32[4]{0:T(128)S(1)} %copy-done.9, s32[4,128]{1,0:T(4,128)S(1)} %copy-done.7, bf16[4,256,256]{2,1,0:T(8,128)(2,1)S(1)} %copy-done.4, bf16[256,512]{1,0:T(8,128)(2,1)S(1)} %bitcast.11), custom_call_target="tpu_custom_call" | custom-call | flops 1048576 | bytes 262144 | tf_op jit(solution)/shard_map/pallas_call | solution.py:240
  106.9 0.0 collective-permute-done.14.a_ref
  106.9 3.6 %collective-permute-done.15.b_ref = bf16[560,256]{1,0:T(8,128)(2,1)S(1)} collective-permute-done((bf16[560,256]{1,0:T(8,128)(2,1)S(1)}, bf16[560,256]{1,0:T(8,128)(2,1)S(1)}, u32[]{:S(2)}, u32[]{:S(2)}) %collective-permute-start.15) | collective-permute-done | bytes 286752 | tf_op jit(solution)/shard_map/ppermute | solution.py:386
  110.6 2.2 %copy-done.2 = bf16[256,8192]{1,0:T(8,128)(2,1)S(1)} copy-done((bf16[256,8192]{1,0:T(8,128)(2,1)S(1)}, bf16[256,8192]{1,0:T(8,128)(2,1)}, u32[]{:S(2)}) %copy-start.2) | copy-done | bytes 4194328
  112.8 1.7 %shard_map.115 = (f32[512,256]{1,0:T(8,128)}, f32[1,8192]{1,0:T(1,128)}, f32[1,1]{1,0:T(1,128)}) custom-call(bf16[512,256]{1,0:T(8,128)(2,1)S(1)} %get-tuple-element.31.near_ref, bf16[560,256]{1,0:T(8,128)(2,1)S(1)} %collective-permute-done.14.a_ref, bf16[560,256]{1,0:T(8,128)(2,1)S(1)} %collective-permute-done.15.b_ref, ...), custom_call_target="tpu_custom_call" | custom-call | flops 100663296 | bytes 5242880 | tf_op jit(solution)/shard_map/pallas_call | solution.py:347
  (16 shorter events, 0.1 us)
Async XLA Ops:
  0.6 1.0 copy-start.3
  1.7 1.0 copy-start.5
  2.7 0.7 copy-start.6
  3.4 0.7 copy-start.8
  5.1 2.0 %collective-permute-start = (bf16[2,528,256]{2,1,0:T(8,128)(2,1)S(1)}, bf16[2,528,256]{2,1,0:T(8,128)(2,1)S(1)}, u32[]{:S(2)}, u32[]{:S(2)}) collective-permute-start(bf16[2,528,256]{2,1,0:T(8,128)(2,1)S(1)} %shard_map.102.mine_ref), channel_id=1, source_target_pairs={{0,16},{16,0},{1,17},{17,1},{2,18},{18,2},{3,19},{19,3},{4,20},{20... | collective-permute-start | bytes 1622024 | tf_op jit(solution)/shard_map/ppermute | solution.py:389
  7.2 2.2 %copy-start = (bf16[256,8192]{1,0:T(8,128)(2,1)S(1)}, bf16[256,8192]{1,0:T(8,128)(2,1)}, u32[]{:S(2)}) copy-start(bf16[256,8192]{1,0:T(8,128)(2,1)} %p_ref.5) | copy-start | bytes 12582916
  9.4 0.8 copy-start.12
  10.1 28.8 %copy-start.13 = (f32[8192]{0:T(1024)S(1)}, f32[8192]{0:T(1024)}, u32[]{:S(2)}) copy-start(f32[8192]{0:T(1024)} %param.10) | copy-start | bytes 98308
  21.5 1.5 %collective-permute-start.1 = (f32[40,128]{1,0:T(8,128)S(1)}, f32[40,128]{1,0:T(8,128)S(1)}, u32[]{:S(2)}, u32[]{:S(2)}) collective-permute-start(f32[40,128]{1,0:T(8,128)S(1)} %get-tuple-element.27.mine_ref), channel_id=1, source_target_pairs={{0,16},{16,0},{1,17},{17,1},{2,18},{18,2},{3,19},{19,3},{4,20},{20... | collective-permute-start | bytes 61448 | tf_op jit(solution)/shard_map/ppermute | solution.py:393
  23.0 4.4 %collective-permute-start.4 = (f32[40,128]{1,0:T(8,128)S(1)}, f32[40,128]{1,0:T(8,128)S(1)}, u32[]{:S(2)}, u32[]{:S(2)}) collective-permute-start(f32[40,128]{1,0:T(8,128)S(1)} %shard_map.104.a), channel_id=1, source_target_pairs={{0,3},{1,2},{2,1},{3,0},{4,7},{5,6},{6,5},{7,4},{8,11},{9,10},{10,... | collective-permute-start | bytes 61448 | tf_op jit(solution)/shard_map/ppermute | solution.py:383
  24.6 5.4 %collective-permute-start.3 = (f32[40,128]{1,0:T(8,128)S(1)}, f32[40,128]{1,0:T(8,128)S(1)}, u32[]{:S(2)}, u32[]{:S(2)}) collective-permute-start(f32[40,128]{1,0:T(8,128)S(1)} %shard_map.104.a), channel_id=1, source_target_pairs={{0,2},{1,3},{2,0},{3,1},{4,6},{5,7},{6,4},{7,5},{8,10},{9,11},{10,... | collective-permute-start | bytes 61448 | tf_op jit(solution)/shard_map/ppermute | solution.py:383
  27.3 3.8 %collective-permute-start.2 = (f32[40,128]{1,0:T(8,128)S(1)}, f32[40,128]{1,0:T(8,128)S(1)}, u32[]{:S(2)}, u32[]{:S(2)}) collective-permute-start(f32[40,128]{1,0:T(8,128)S(1)} %shard_map.104.a), channel_id=1, source_target_pairs={{0,1},{1,0},{2,3},{3,2},{4,5},{5,4},{6,7},{7,6},{8,9},{9,8},{10,11... | collective-permute-start | bytes 61448 | tf_op jit(solution)/shard_map/ppermute | solution.py:383
  31.1 5.1 %collective-permute-start.7 = (f32[40,128]{1,0:T(8,128)S(1)}, f32[40,128]{1,0:T(8,128)S(1)}, u32[]{:S(2)}, u32[]{:S(2)}) collective-permute-start(f32[40,128]{1,0:T(8,128)S(1)} %shard_map.105.a), channel_id=1, source_target_pairs={{0,12},{4,8},{8,4},{12,0},{1,13},{5,9},{9,5},{13,1},{2,14},{6,10},... | collective-permute-start | bytes 61448 | tf_op jit(solution)/shard_map/ppermute | solution.py:383
  32.9 5.3 %collective-permute-start.6 = (f32[40,128]{1,0:T(8,128)S(1)}, f32[40,128]{1,0:T(8,128)S(1)}, u32[]{:S(2)}, u32[]{:S(2)}) collective-permute-start(f32[40,128]{1,0:T(8,128)S(1)} %shard_map.105.a), channel_id=1, source_target_pairs={{0,8},{4,12},{8,0},{12,4},{1,9},{5,13},{9,1},{13,5},{2,10},{6,14},... | collective-permute-start | bytes 61448 | tf_op jit(solution)/shard_map/ppermute | solution.py:383
  33.7 4.5 %collective-permute-start.5 = (f32[40,128]{1,0:T(8,128)S(1)}, f32[40,128]{1,0:T(8,128)S(1)}, u32[]{:S(2)}, u32[]{:S(2)}) collective-permute-start(f32[40,128]{1,0:T(8,128)S(1)} %shard_map.105.a), channel_id=1, source_target_pairs={{0,4},{4,0},{8,12},{12,8},{1,5},{5,1},{9,13},{13,9},{2,6},{6,2},{1... | collective-permute-start | bytes 61448 | tf_op jit(solution)/shard_map/ppermute | solution.py:383
  38.9 2.2 %copy-start.1 = (bf16[256,8192]{1,0:T(8,128)(2,1)S(1)}, bf16[256,8192]{1,0:T(8,128)(2,1)}, u32[]{:S(2)}) copy-start(bf16[256,8192]{1,0:T(8,128)(2,1)} %p_ref.5) | copy-start | bytes 12582916
  52.1 0.7 copy-start.10
  52.8 0.6 copy-start.11
  53.4 49.3 %copy-start.4 = (bf16[4,256,256]{2,1,0:T(8,128)(2,1)S(1)}, bf16[4,256,256]{2,1,0:T(8,128)(2,1)}, u32[]{:S(2)}) copy-start(bf16[4,256,256]{2,1,0:T(8,128)(2,1)} %s_ref.3) | copy-start | bytes 1572868
  53.4 19.2 %all-to-all-start = ((bf16[32,16,512]{2,1,0:T(8,128)(2,1)}), bf16[32,16,512]{2,1,0:T(8,128)(2,1)S(1)}, u32[]{:S(2)}, u32[]{:S(2)}) async-start(bf16[32,16,512]{2,1,0:T(8,128)(2,1)} %bitcast.6), calls=%async_computation | async-start | bytes 1048576 | tf_op jit(solution)/shard_map/all_to_all | solution.py:406
  60.2 12.4 %collective-permute-start.8 = (bf16[304,256]{1,0:T(8,128)(2,1)}, bf16[304,256]{1,0:T(8,128)(2,1)S(1)}, u32[]{:S(2)}, u32[]{:S(2)}) collective-permute-start(bf16[304,256]{1,0:T(8,128)(2,1)} %copy-done.10), channel_id=1, source_target_pairs={{0,224},{16,48},{32,0},{48,80},{64,32},{80,112},{96,64},{112,144},... | collective-permute-start | bytes 466952 | tf_op jit(solution)/shard_map/ppermute | solution.py:386
  66.2 6.4 %collective-permute-start.9 = (bf16[256,256]{1,0:T(8,128)(2,1)}, bf16[256,256]{1,0:T(8,128)(2,1)S(1)}, u32[]{:S(2)}, u32[]{:S(2)}) collective-permute-start(bf16[256,256]{1,0:T(8,128)(2,1)} %copy-done.11), channel_id=1, source_target_pairs={{0,32},{16,240},{32,64},{48,16},{64,96},{80,48},{96,128},{112,80},... | collective-permute-start | bytes 393224 | tf_op jit(solution)/shard_map/ppermute | solution.py:386
  73.5 10.1 %collective-permute-start.10 = (bf16[560,256]{1,0:T(8,128)(2,1)S(1)}, bf16[560,256]{1,0:T(8,128)(2,1)S(1)}, u32[]{:S(2)}, u32[]{:S(2)}) collective-permute-start(bf16[560,256]{1,0:T(8,128)(2,1)S(1)} %shard_map.108), channel_id=1, source_target_pairs={{0,224},{16,48},{32,0},{48,80},{64,32},{80,112},{96,64},{112,144},... | collective-permute-start | bytes 860168 | tf_op jit(solution)/shard_map/ppermute | solution.py:386
  77.3 10.1 %collective-permute-start.12 = (bf16[560,256]{1,0:T(8,128)(2,1)S(1)}, bf16[560,256]{1,0:T(8,128)(2,1)S(1)}, u32[]{:S(2)}, u32[]{:S(2)}) collective-permute-start(bf16[560,256]{1,0:T(8,128)(2,1)S(1)} %shard_map.109), channel_id=1, source_target_pairs={{0,32},{16,240},{32,64},{48,16},{64,96},{80,48},{96,128},{112,80},... | collective-permute-start | bytes 860168 | tf_op jit(solution)/shard_map/ppermute | solution.py:386
  83.7 9.2 %collective-permute-start.11 = (bf16[560,256]{1,0:T(8,128)(2,1)S(1)}, bf16[560,256]{1,0:T(8,128)(2,1)S(1)}, u32[]{:S(2)}, u32[]{:S(2)}) collective-permute-start(bf16[560,256]{1,0:T(8,128)(2,1)S(1)} %shard_map.111), channel_id=1, source_target_pairs={{0,224},{16,48},{32,0},{48,80},{64,32},{80,112},{96,64},{112,144},... | collective-permute-start | bytes 860168 | tf_op jit(solution)/shard_map/ppermute | solution.py:386
  87.5 7.9 %collective-permute-start.13 = (bf16[560,256]{1,0:T(8,128)(2,1)S(1)}, bf16[560,256]{1,0:T(8,128)(2,1)S(1)}, u32[]{:S(2)}, u32[]{:S(2)}) collective-permute-start(bf16[560,256]{1,0:T(8,128)(2,1)S(1)} %shard_map.113), channel_id=1, source_target_pairs={{0,32},{16,240},{32,64},{48,16},{64,96},{80,48},{96,128},{112,80},... | collective-permute-start | bytes 860168 | tf_op jit(solution)/shard_map/ppermute | solution.py:386
  87.6 11.9 %all-to-all-start.1 = ((bf16[16,16,512]{2,1,0:T(8,128)(2,1)}), bf16[16,16,512]{2,1,0:T(8,128)(2,1)S(1)}, u32[]{:S(2)}, u32[]{:S(2)}) async-start(bf16[16,16,512]{2,1,0:T(8,128)(2,1)} %shard_map.110), calls=%async_computation.1 | async-start | bytes 524288 | tf_op jit(solution)/shard_map/all_to_all | solution.py:418
  99.5 7.4 %collective-permute-start.14 = (bf16[560,256]{1,0:T(8,128)(2,1)S(1)}, bf16[560,256]{1,0:T(8,128)(2,1)S(1)}, u32[]{:S(2)}, u32[]{:S(2)}) collective-permute-start(bf16[560,256]{1,0:T(8,128)(2,1)S(1)} %shard_map.112), channel_id=1, source_target_pairs={{0,224},{16,48},{32,0},{48,80},{64,32},{80,112},{96,64},{112,144},... | collective-permute-start | bytes 860168 | tf_op jit(solution)/shard_map/ppermute | solution.py:386
  102.7 7.8 %collective-permute-start.15 = (bf16[560,256]{1,0:T(8,128)(2,1)S(1)}, bf16[560,256]{1,0:T(8,128)(2,1)S(1)}, u32[]{:S(2)}, u32[]{:S(2)}) collective-permute-start(bf16[560,256]{1,0:T(8,128)(2,1)S(1)} %shard_map.114), channel_id=1, source_target_pairs={{0,32},{16,240},{32,64},{48,16},{64,96},{80,48},{96,128},{112,80},... | collective-permute-start | bytes 860168 | tf_op jit(solution)/shard_map/ppermute | solution.py:386
  102.7 0.7 copy-start.7
  103.4 0.7 copy-start.9
  110.6 2.2 %copy-start.2 = (bf16[256,8192]{1,0:T(8,128)(2,1)S(1)}, bf16[256,8192]{1,0:T(8,128)(2,1)}, u32[]{:S(2)}) copy-start(bf16[256,8192]{1,0:T(8,128)(2,1)} %p_ref.5) | copy-start | bytes 12582916
where the time goes:
time: 115 us
  starting transfers between devices  37.6 us (33%)
  waiting for transfers between devices  32.1 us (28%)
  Pallas kernels  29.8 us (26%)
  local copies, waits for them, and re-layouts  13.4 us (12%)
  between operations  1.6 us (1%)
    ppermute x8, waiting for transfers between devices, ring(): return lax.ppermute(value, ('z', 'core'), pairs)  19.2 us
    ppermute x8, starting transfers between devices, ring(): return lax.ppermute(value, ('z', 'core'), pairs)  16.8 us
    unnamed x28, local copies, waits for them, and re-layouts  13.4 us
    pallas_call x1, Pallas kernels, local_stats(): pl.pallas_call(stats_kernel, in_specs=[smem, vmem, vmem, vmem, vmem], out...  11.4 us
    pallas_call x1, Pallas kernels, grads(): pl.pallas_call(grad_kernel, in_specs=[smem] + [vmem] * 6, out_specs=[vmem...  11.1 us
    ppermute x6, starting transfers between devices, swaps(): lax.ppermute(value, axis, [(i, i ^ k) for i in range(4)])  8.53 us
    all_to_all x1, starting transfers between devices, shards(): got = lax.all_to_all(send.reshape(PEERS, part, ROWS), peers, 0, 0)  6.79 us
    ppermute x6, waiting for transfers between devices, swaps(): lax.ppermute(value, axis, [(i, i ^ k) for i in range(4)])  6.04 us
  transfers between devices with their start and end apart: 18, of which 12 were waited for; matrix products, arithmetic and copies ran while one was open for 0% of the time, Pallas kernels for 3%

commit v1 on v0

--- a/solution.py
+++ b/solution.py
@@ -29,7 +29,7 @@
 CHUNK = 512
 TILE = 512
 STAT_TILE = 256
-EXTRA = 48
+EXTRA = 32
 HELD = ROWS + 16
 STATS = 5
 PEERS = CORES * X * Y
@@ -226,9 +226,9 @@
     row_sum = split3(sum_ref[0:1, :])
     losses = split3(jnp.broadcast_to(first + second, (1, D)))
     block = jnp.zeros((EXTRA, D), f32)
-    for i in range(3):
+    for i in range(2):
         block = jnp.where(row // Z == i, row_sum[i].astype(f32), block)
-        block = jnp.where(row // Z == 3 + i, losses[i].astype(f32), block)
+        block = jnp.where(row // Z == 2 + i, losses[i].astype(f32), block)
     misc_ref[...] = jnp.where(mine, block, 0.0).astype(bf16)
 
 
@@ -330,8 +330,8 @@
     total = near_ref[...].astype(f32) + a_ref[:CHUNK, :].astype(f32)
     grad_ref[...] = total + b_ref[:CHUNK, :].astype(f32)
     extra = (misc_ref[...] + a_ref[CHUNK:, :] + b_ref[CHUNK:, :]).astype(f32)
-    first = extra[0:8] + extra[8:16] + extra[16:24]
-    loss = extra[24:32] + extra[32:40] + extra[40:48]
+    first = extra[0:8] + extra[8:16]
+    loss = extra[16:24] + extra[24:32]
     total = jnp.broadcast_to(jnp.sum(first, axis=0, keepdims=True), (16, D))
     loss_ref[0, 0] = jnp.sum(loss[:, 0:1])
     stacked = jnp.concatenate(split3(total), axis=0)
@@ -405,6 +405,7 @@
     part = D // (X * Y)
     got = lax.all_to_all(send.reshape(PEERS, part, ROWS), peers, 0, 0)
     own = small_call(du_sum_kernel, jax.ShapeDtypeStruct((X * Y, part, ROWS), bf16), got)
+    du = lax.all_to_all(own, ("x", "y"), 0, 0)
     for i in range(3):
         if i == 0:
             kernel_a = functools.partial(halves_kernel, 0, True)
@@ -413,9 +414,6 @@
             kernel_a = kernel_b = step_kernel
         send_a = small_call(kernel_a, step_shape, near[2 * i], got_a, misc)
         send_b = small_call(kernel_b, step_shape, near[2 * i + 1], got_b, misc)
-        if i == 0:
-            send_a, send_b, own = lax.optimization_barrier((send_a, send_b, own))
-            du = lax.all_to_all(own, ("x", "y"), 0, 0)
         if i == 2:
             send_a, send_b, du = lax.optimization_barrier((send_a, send_b, du))
         got_a, got_b = ring(send_a, one_way), ring(send_b, other_way)

time: 115 us -> 113 us (0.983)
  local copies, waits for them, and re-layouts: 13.4 us -> 12.1 us
    ppermute x8, waiting for transfers between devices: 19.2 us -> 15.6 us  [ring(): return lax.ppermute(value, ('z', 'core'), pairs)]
    all_to_all x1, waiting for transfers between devices: 4.01 us -> 6.82 us  [shards(): du = lax.all_to_all(own, ('x', 'y'), 0, 0)]
    all_to_all x1, starting transfers between devices: 4.93 us -> 7.27 us  [shards(): du = lax.all_to_all(own, ('x', 'y'), 0, 0)]
    ppermute x8, starting transfers between devices: 16.8 us -> 15 us  [ring(): return lax.ppermute(value, ('z', 'core'), pairs)]
    unnamed x28, local copies, waits for them, and re-layouts: 13.4 us -> 12.1 us
  transfers between devices with their start and end apart: 18 -> 18, of which waited for: 12 -> 11; matrix products, arithmetic and copies ran while one was open for 0% -> 0% of each run, Pallas kernels for 3% -> 4%
where the time goes in v1:
time: 113 us
  starting transfers between devices  38.1 us (34%)
  waiting for transfers between devices  31.4 us (28%)
  Pallas kernels  29.5 us (26%)
  local copies, waits for them, and re-layouts  12.1 us (11%)
  between operations  1.66 us (1%)
    ppermute x8, waiting for transfers between devices, ring(): return lax.ppermute(value, ('z', 'core'), pairs)  15.6 us
    ppermute x8, starting transfers between devices, ring(): return lax.ppermute(value, ('z', 'core'), pairs)  15 us
    unnamed x28, local copies, waits for them, and re-layouts  12.1 us
    pallas_call x1, Pallas kernels, local_stats(): pl.pallas_call(stats_kernel, in_specs=[smem, vmem, vmem, vmem, vmem], out...  11.2 us
    pallas_call x1, Pallas kernels, grads(): pl.pallas_call(grad_kernel, in_specs=[smem] + [vmem] * 6, out_specs=[vmem...  10.9 us
    ppermute x6, starting transfers between devices, swaps(): lax.ppermute(value, axis, [(i, i ^ k) for i in range(4)])  8.53 us
    all_to_all x1, starting transfers between devices, shards(): du = lax.all_to_all(own, ('x', 'y'), 0, 0)  7.27 us
    all_to_all x1, waiting for transfers between devices, shards(): du = lax.all_to_all(own, ('x', 'y'), 0, 0)  6.82 us
  transfers between devices with their start and end apart: 18, of which 11 were waited for; matrix products, arithmetic and copies ran while one was open for 0% of the time, Pallas kernels for 4%

profile of v1, /device:TPU:8, one launch (start us, length us, event | category | flops | bytes accessed | tf_op | source)
XLA Modules:
  0.0 112.7 jit_solution(9641507863590713646)
XLA Ops:
  0.6 0.0 copy-start.3
  0.6 1.0 copy-done.3
  1.7 1.0 copy-done.5
  2.7 0.7 copy-done.6
  3.4 0.7 copy-done.8
  4.1 1.1 shard_map.102.mine_ref
  5.1 0.1 collective-permute-start
  5.2 0.1 pad_add_fusion.ids_ref
  5.3 1.8 %collective-permute-done.other_ref = bf16[2,528,256]{2,1,0:T(8,128)(2,1)S(1)} collective-permute-done((bf16[2,528,256]{2,1,0:T(8,128)(2,1)S(1)}, bf16[2,528,256]{2,1,0:T(8,128)(2,1)S(1)}, u32[]{:S(2)}, u32[]{:S(2)}) %collective-permute-start) | collective-permute-done | bytes 540704 | tf_op jit(solution)/shard_map/ppermute | solution.py:389
  7.2 2.2 %copy-done = bf16[256,8192]{1,0:T(8,128)(2,1)S(1)} copy-done((bf16[256,8192]{1,0:T(8,128)(2,1)S(1)}, bf16[256,8192]{1,0:T(8,128)(2,1)}, u32[]{:S(2)}) %copy-start) | copy-done | bytes 4194328
  9.4 0.8 copy-done.12
  10.1 11.2 %shard_map.103 = (f32[40,128]{1,0:T(8,128)S(1)}, f32[8,256]{1,0:T(8,128)S(1)}) custom-call(s32[4]{0:T(128)S(1)} %pad_add_fusion.ids_ref, bf16[256,8192]{1,0:T(8,128)(2,1)S(1)} %copy-done, f32[1,8192]{1,0:T(1,128)S(1)} %bitcast.12, bf16[2,528,256]{2,1,0:T(8,128)(2,1)S(1)} %shard_map.102.mine_ref, bf16[2,528,256]{2,1,0:T(8,128)(2,1)S(1)} %collective-permute-done.other_ref), custom_call_target="tpu_custom_call" | custom-call | flops 4294967296 | bytes 6291456 | tf_op jit(solution)/shard_map/pallas_call | solution.py:151
  21.3 0.4 collective-permute-start.1
  21.7 1.1 collective-permute-done.1.got_ref
  22.8 1.7 %collective-permute-start.4 = (f32[40,128]{1,0:T(8,128)S(1)}, f32[40,128]{1,0:T(8,128)S(1)}, u32[]{:S(2)}, u32[]{:S(2)}) collective-permute-start(f32[40,128]{1,0:T(8,128)S(1)} %shard_map.104.a), channel_id=1, source_target_pairs={{0,3},{1,2},{2,1},{3,0},{4,7},{5,6},{6,5},{7,4},{8,11},{9,10},{10,... | collective-permute-start | bytes 61448 | tf_op jit(solution)/shard_map/ppermute | solution.py:383
  24.5 2.7 %collective-permute-start.3 = (f32[40,128]{1,0:T(8,128)S(1)}, f32[40,128]{1,0:T(8,128)S(1)}, u32[]{:S(2)}, u32[]{:S(2)}) collective-permute-start(f32[40,128]{1,0:T(8,128)S(1)} %shard_map.104.a), channel_id=1, source_target_pairs={{0,2},{1,3},{2,0},{3,1},{4,6},{5,7},{6,4},{7,5},{8,10},{9,11},{10,... | collective-permute-start | bytes 61448 | tf_op jit(solution)/shard_map/ppermute | solution.py:383
  27.1 0.0 collective-permute-start.2
  27.1 0.0 collective-permute-done.4.d
  27.1 2.7 %collective-permute-done.3.c = f32[40,128]{1,0:T(8,128)S(1)} collective-permute-done((f32[40,128]{1,0:T(8,128)S(1)}, f32[40,128]{1,0:T(8,128)S(1)}, u32[]{:S(2)}, u32[]{:S(2)}) %collective-permute-start.3) | collective-permute-done | bytes 20512 | tf_op jit(solution)/shard_map/ppermute | solution.py:383
  29.9 1.0 collective-permute-done.2.b
  30.9 1.8 %collective-permute-start.7 = (f32[40,128]{1,0:T(8,128)S(1)}, f32[40,128]{1,0:T(8,128)S(1)}, u32[]{:S(2)}, u32[]{:S(2)}) collective-permute-start(f32[40,128]{1,0:T(8,128)S(1)} %shard_map.105.a), channel_id=1, source_target_pairs={{0,12},{4,8},{8,4},{12,0},{1,13},{5,9},{9,5},{13,1},{2,14},{6,10},... | collective-permute-start | bytes 61448 | tf_op jit(solution)/shard_map/ppermute | solution.py:383
  32.7 0.8 collective-permute-start.6
  33.6 1.6 %collective-permute-start.5 = (f32[40,128]{1,0:T(8,128)S(1)}, f32[40,128]{1,0:T(8,128)S(1)}, u32[]{:S(2)}, u32[]{:S(2)}) collective-permute-start(f32[40,128]{1,0:T(8,128)S(1)} %shard_map.105.a), channel_id=1, source_target_pairs={{0,4},{4,0},{8,12},{12,8},{1,5},{5,1},{9,13},{13,9},{2,6},{6,2},{1... | collective-permute-start | bytes 61448 | tf_op jit(solution)/shard_map/ppermute | solution.py:383
  35.8 0.2 collective-permute-done.7.d
  36.0 2.0 %collective-permute-done.6.c = f32[40,128]{1,0:T(8,128)S(1)} collective-permute-done((f32[40,128]{1,0:T(8,128)S(1)}, f32[40,128]{1,0:T(8,128)S(1)}, u32[]{:S(2)}, u32[]{:S(2)}) %collective-permute-start.6) | collective-permute-done | bytes 20512 | tf_op jit(solution)/shard_map/ppermute | solution.py:383
  38.0 0.0 collective-permute-done.5.b
  38.0 0.7 shard_map.106
  38.7 0.0 copy-done.13
  38.7 0.0 copy-start.1
  38.7 2.2 %copy-done.1 = bf16[256,8192]{1,0:T(8,128)(2,1)S(1)} copy-done((bf16[256,8192]{1,0:T(8,128)(2,1)S(1)}, bf16[256,8192]{1,0:T(8,128)(2,1)}, u32[]{:S(2)}) %copy-start.1) | copy-done | bytes 4194328
  40.9 10.9 %shard_map.107 = (bf16[288,256]{1,0:T(8,128)(2,1)S(1)}, bf16[256,256]{1,0:T(8,128)(2,1)S(1)}, bf16[512,256]{1,0:T(8,128)(2,1)S(1)}, bf16[512,256]{1,0:T(8,128)(2...) custom-call(s32[4]{0:T(128)S(1)} %pad_add_fusion.ids_ref, ...), custom_call_target="tpu_custom_call" | custom-call | flops 8589934592 | bytes 8388608 | tf_op jit(solution)/shard_map/pallas_call | solution.py:292
  51.8 0.7 copy-done.10
  52.5 0.6 copy-done.11
  53.1 6.8 %all-to-all-start = ((bf16[32,16,512]{2,1,0:T(8,128)(2,1)}), bf16[32,16,512]{2,1,0:T(8,128)(2,1)S(1)}, u32[]{:S(2)}, u32[]{:S(2)}) async-start(bf16[32,16,512]{2,1,0:T(8,128)(2,1)} %bitcast.6), calls=%async_computation | async-start | bytes 1048576 | tf_op jit(solution)/shard_map/all_to_all | solution.py:406
  59.9 5.9 %collective-permute-start.8 = (bf16[288,256]{1,0:T(8,128)(2,1)}, bf16[288,256]{1,0:T(8,128)(2,1)S(1)}, u32[]{:S(2)}, u32[]{:S(2)}) collective-permute-start(bf16[288,256]{1,0:T(8,128)(2,1)} %copy-done.10), channel_id=1, source_target_pairs={{0,224},{16,48},{32,0},{48,80},{64,32},{80,112},{96,64},{112,144},... | collective-permute-start | bytes 442376 | tf_op jit(solution)/shard_map/ppermute | solution.py:386
  65.8 0.0 collective-permute-start.11
  65.9 6.4 %collective-permute-done.11.got_ref = bf16[256,256]{1,0:T(8,128)(2,1)S(1)} collective-permute-done((bf16[256,256]{1,0:T(8,128)(2,1)}, bf16[256,256]{1,0:T(8,128)(2,1)S(1)}, u32[]{:S(2)}, u32[]{:S(2)}) %collective-permute-start.11) | collective-permute-done | bytes 131104 | tf_op jit(solution)/shard_map/ppermute | solution.py:386
  72.3 0.3 collective-permute-start.12
  72.6 0.0 collective-permute-done.8.got_ref
  72.7 3.3 %collective-permute-start.9 = (bf16[544,256]{1,0:T(8,128)(2,1)S(1)}, bf16[544,256]{1,0:T(8,128)(2,1)S(1)}, u32[]{:S(2)}, u32[]{:S(2)}) collective-permute-start(bf16[544,256]{1,0:T(8,128)(2,1)S(1)} %shard_map.108), channel_id=1, source_target_pairs={{0,224},{16,48},{32,0},{48,80},{64,32},{80,112},{96,64},{112,144},... | collective-permute-start | bytes 835592 | tf_op jit(solution)/shard_map/ppermute | solution.py:386
  76.0 6.3 %collective-permute-done.12.got_ref = bf16[544,256]{1,0:T(8,128)(2,1)S(1)} collective-permute-done((bf16[544,256]{1,0:T(8,128)(2,1)S(1)}, bf16[544,256]{1,0:T(8,128)(2,1)S(1)}, u32[]{:S(2)}, u32[]{:S(2)}) %collective-permute-start.12) | collective-permute-done | bytes 278560 | tf_op jit(solution)/shard_map/ppermute | solution.py:386
  82.3 0.1 shard_map.112
  82.4 0.1 collective-permute-start.13
  82.5 0.0 collective-permute-done.9.got_ref
  82.5 0.1 shard_map.109
  82.6 3.3 %collective-permute-start.10 = (bf16[544,256]{1,0:T(8,128)(2,1)S(1)}, bf16[544,256]{1,0:T(8,128)(2,1)S(1)}, u32[]{:S(2)}, u32[]{:S(2)}) collective-permute-start(bf16[544,256]{1,0:T(8,128)(2,1)S(1)} %shard_map.109), channel_id=1, source_target_pairs={{0,224},{16,48},{32,0},{48,80},{64,32},{80,112},{96,64},{112,144},... | collective-permute-start | bytes 835592 | tf_op jit(solution)/shard_map/ppermute | solution.py:386
  85.8 0.0 all-to-all-done.got_ref
  85.9 0.8 shard_map.114
  86.6 7.3 %all-to-all-start.1 = ((bf16[16,16,512]{2,1,0:T(8,128)(2,1)}), bf16[16,16,512]{2,1,0:T(8,128)(2,1)S(1)}, u32[]{:S(2)}, u32[]{:S(2)}) async-start(bf16[16,16,512]{2,1,0:T(8,128)(2,1)} %shard_map.114), calls=%async_computation.1 | async-start | bytes 524288 | tf_op jit(solution)/shard_map/all_to_all | solution.py:408
  93.9 0.0 collective-permute-done.13.got_ref
  93.9 0.1 shard_map.113
  94.0 0.0 collective-permute-done.10.got_ref
  94.0 0.1 shard_map.110
  94.1 6.8 %all-to-all-done.1 = bf16[16,16,512]{2,1,0:T(8,128)(2,1)S(1)} async-done(((bf16[16,16,512]{2,1,0:T(8,128)(2,1)}), bf16[16,16,512]{2,1,0:T(8,128)(2,1)S(1)}, u32[]{:S(2)}, u32[]{:S(2)}) %all-to-all-start.1) | async-done | bytes 262176 | tf_op jit(solution)/shard_map/all_to_all | solution.py:408
  100.9 0.0 collective-permute-start.14
  100.9 2.0 %collective-permute-start.15 = (bf16[544,256]{1,0:T(8,128)(2,1)S(1)}, bf16[544,256]{1,0:T(8,128)(2,1)S(1)}, u32[]{:S(2)}, u32[]{:S(2)}) collective-permute-start(bf16[544,256]{1,0:T(8,128)(2,1)S(1)} %shard_map.113), channel_id=1, source_target_pairs={{0,32},{16,240},{32,64},{48,16},{64,96},{80,48},{96,128},{112,80},... | collective-permute-start | bytes 835592 | tf_op jit(solution)/shard_map/ppermute | solution.py:386
  102.9 0.0 copy-done.4
  102.9 0.0 copy-done.7
  102.9 0.0 copy-done.9
  102.9 2.9 %shard_map.116 = f32[4,256,256]{2,1,0:T(8,128)} custom-call(s32[4]{0:T(128)S(1)} %copy-done.9, s32[4,128]{1,0:T(4,128)S(1)} %copy-done.7, bf16[4,256,256]{2,1,0:T(8,128)(2,1)S(1)} %copy-done.4, bf16[256,512]{1,0:T(8,128)(2,1)S(1)} %bitcast.11), custom_call_target="tpu_custom_call" | custom-call | flops 1048576 | bytes 262144 | tf_op jit(solution)/shard_map/pallas_call | solution.py:240
  105.8 1.6 %collective-permute-done.14.a_ref = bf16[544,256]{1,0:T(8,128)(2,1)S(1)} collective-permute-done((bf16[544,256]{1,0:T(8,128)(2,1)S(1)}, bf16[544,256]{1,0:T(8,128)(2,1)S(1)}, u32[]{:S(2)}, u32[]{:S(2)}) %collective-permute-start.14) | collective-permute-done | bytes 278560 | tf_op jit(solution)/shard_map/ppermute | solution.py:386
  107.5 1.2 %collective-permute-done.15.b_ref = bf16[544,256]{1,0:T(8,128)(2,1)S(1)} collective-permute-done((bf16[544,256]{1,0:T(8,128)(2,1)S(1)}, bf16[544,256]{1,0:T(8,128)(2,1)S(1)}, u32[]{:S(2)}, u32[]{:S(2)}) %collective-permute-start.15) | collective-permute-done | bytes 278560 | tf_op jit(solution)/shard_map/ppermute | solution.py:386
  108.7 2.2 %copy-done.2 = bf16[256,8192]{1,0:T(8,128)(2,1)S(1)} copy-done((bf16[256,8192]{1,0:T(8,128)(2,1)S(1)}, bf16[256,8192]{1,0:T(8,128)(2,1)}, u32[]{:S(2)}) %copy-start.2) | copy-done | bytes 4194328
  110.9 1.7 %shard_map.115 = (f32[512,256]{1,0:T(8,128)}, f32[1,8192]{1,0:T(1,128)}, f32[1,1]{1,0:T(1,128)}) custom-call(bf16[512,256]{1,0:T(8,128)(2,1)S(1)} %get-tuple-element.28.near_ref, bf16[544,256]{1,0:T(8,128)(2,1)S(1)} %collective-permute-done.14.a_ref, bf16[544,256]{1,0:T(8,128)(2,1)S(1)} %collective-permute-done.15.b_ref, ...), custom_call_target="tpu_custom_call" | custom-call | flops 100663296 | bytes 5242880 | tf_op jit(solution)/shard_map/pallas_call | solution.py:347
  (16 shorter events, 0.1 us)
Async XLA Ops:
  0.6 1.0 copy-start.3
  1.7 1.0 copy-start.5
  2.7 0.7 copy-start.6
  3.4 0.7 copy-start.8
  5.1 2.0 %collective-permute-start = (bf16[2,528,256]{2,1,0:T(8,128)(2,1)S(1)}, bf16[2,528,256]{2,1,0:T(8,128)(2,1)S(1)}, u32[]{:S(2)}, u32[]{:S(2)}) collective-permute-start(bf16[2,528,256]{2,1,0:T(8,128)(2,1)S(1)} %shard_map.102.mine_ref), channel_id=1, source_target_pairs={{0,16},{16,0},{1,17},{17,1},{2,18},{18,2},{3,19},{19,3},{4,20},{20... | collective-permute-start | bytes 1622024 | tf_op jit(solution)/shard_map/ppermute | solution.py:389
  7.2 2.2 %copy-start = (bf16[256,8192]{1,0:T(8,128)(2,1)S(1)}, bf16[256,8192]{1,0:T(8,128)(2,1)}, u32[]{:S(2)}) copy-start(bf16[256,8192]{1,0:T(8,128)(2,1)} %p_ref.5) | copy-start | bytes 12582916
  9.4 0.8 copy-start.12
  10.1 28.6 %copy-start.13 = (f32[8192]{0:T(1024)S(1)}, f32[8192]{0:T(1024)}, u32[]{:S(2)}) copy-start(f32[8192]{0:T(1024)} %param.10) | copy-start | bytes 98308
  21.3 1.5 %collective-permute-start.1 = (f32[40,128]{1,0:T(8,128)S(1)}, f32[40,128]{1,0:T(8,128)S(1)}, u32[]{:S(2)}, u32[]{:S(2)}) collective-permute-start(f32[40,128]{1,0:T(8,128)S(1)} %get-tuple-element.24.mine_ref), channel_id=1, source_target_pairs={{0,16},{16,0},{1,17},{17,1},{2,18},{18,2},{3,19},{19,3},{4,20},{20... | collective-permute-start | bytes 61448 | tf_op jit(solution)/shard_map/ppermute | solution.py:393
  22.8 4.4 %collective-permute-start.4 = (f32[40,128]{1,0:T(8,128)S(1)}, f32[40,128]{1,0:T(8,128)S(1)}, u32[]{:S(2)}, u32[]{:S(2)}) collective-permute-start(f32[40,128]{1,0:T(8,128)S(1)} %shard_map.104.a), channel_id=1, source_target_pairs={{0,3},{1,2},{2,1},{3,0},{4,7},{5,6},{6,5},{7,4},{8,11},{9,10},{10,... | collective-permute-start | bytes 61448 | tf_op jit(solution)/shard_map/ppermute | solution.py:383
  24.5 5.4 %collective-permute-start.3 = (f32[40,128]{1,0:T(8,128)S(1)}, f32[40,128]{1,0:T(8,128)S(1)}, u32[]{:S(2)}, u32[]{:S(2)}) collective-permute-start(f32[40,128]{1,0:T(8,128)S(1)} %shard_map.104.a), channel_id=1, source_target_pairs={{0,2},{1,3},{2,0},{3,1},{4,6},{5,7},{6,4},{7,5},{8,10},{9,11},{10,... | collective-permute-start | bytes 61448 | tf_op jit(solution)/shard_map/ppermute | solution.py:383
  27.1 3.8 %collective-permute-start.2 = (f32[40,128]{1,0:T(8,128)S(1)}, f32[40,128]{1,0:T(8,128)S(1)}, u32[]{:S(2)}, u32[]{:S(2)}) collective-permute-start(f32[40,128]{1,0:T(8,128)S(1)} %shard_map.104.a), channel_id=1, source_target_pairs={{0,1},{1,0},{2,3},{3,2},{4,5},{5,4},{6,7},{7,6},{8,9},{9,8},{10,11... | collective-permute-start | bytes 61448 | tf_op jit(solution)/shard_map/ppermute | solution.py:383
  30.9 5.1 %collective-permute-start.7 = (f32[40,128]{1,0:T(8,128)S(1)}, f32[40,128]{1,0:T(8,128)S(1)}, u32[]{:S(2)}, u32[]{:S(2)}) collective-permute-start(f32[40,128]{1,0:T(8,128)S(1)} %shard_map.105.a), channel_id=1, source_target_pairs={{0,12},{4,8},{8,4},{12,0},{1,13},{5,9},{9,5},{13,1},{2,14},{6,10},... | collective-permute-start | bytes 61448 | tf_op jit(solution)/shard_map/ppermute | solution.py:383
  32.7 5.3 %collective-permute-start.6 = (f32[40,128]{1,0:T(8,128)S(1)}, f32[40,128]{1,0:T(8,128)S(1)}, u32[]{:S(2)}, u32[]{:S(2)}) collective-permute-start(f32[40,128]{1,0:T(8,128)S(1)} %shard_map.105.a), channel_id=1, source_target_pairs={{0,8},{4,12},{8,0},{12,4},{1,9},{5,13},{9,1},{13,5},{2,10},{6,14},... | collective-permute-start | bytes 61448 | tf_op jit(solution)/shard_map/ppermute | solution.py:383
  33.6 4.5 %collective-permute-start.5 = (f32[40,128]{1,0:T(8,128)S(1)}, f32[40,128]{1,0:T(8,128)S(1)}, u32[]{:S(2)}, u32[]{:S(2)}) collective-permute-start(f32[40,128]{1,0:T(8,128)S(1)} %shard_map.105.a), channel_id=1, source_target_pairs={{0,4},{4,0},{8,12},{12,8},{1,5},{5,1},{9,13},{13,9},{2,6},{6,2},{1... | collective-permute-start | bytes 61448 | tf_op jit(solution)/shard_map/ppermute | solution.py:383
  38.7 2.2 %copy-start.1 = (bf16[256,8192]{1,0:T(8,128)(2,1)S(1)}, bf16[256,8192]{1,0:T(8,128)(2,1)}, u32[]{:S(2)}) copy-start(bf16[256,8192]{1,0:T(8,128)(2,1)} %p_ref.5) | copy-start | bytes 12582916
  51.8 0.7 copy-start.10
  52.5 0.6 copy-start.11
  53.1 49.8 %copy-start.4 = (bf16[4,256,256]{2,1,0:T(8,128)(2,1)S(1)}, bf16[4,256,256]{2,1,0:T(8,128)(2,1)}, u32[]{:S(2)}) copy-start(bf16[4,256,256]{2,1,0:T(8,128)(2,1)} %s_ref.3) | copy-start | bytes 1572868
  53.1 49.8 %copy-start.7 = (s32[4,128]{1,0:T(4,128)S(1)}, s32[4,128]{1,0:T(4,128)}, u32[]{:S(2)}) copy-start(s32[4,128]{1,0:T(4,128)} %index_ref.3) | copy-start | bytes 6148
  53.1 49.8 %copy-start.9 = (s32[4]{0:T(128)S(1)}, s32[4]{0:T(128)}, u32[]{:S(2)}) copy-start(s32[4]{0:T(128)} %count_ref.3) | copy-start | bytes 52
  53.1 32.7 %all-to-all-start = ((bf16[32,16,512]{2,1,0:T(8,128)(2,1)}), bf16[32,16,512]{2,1,0:T(8,128)(2,1)S(1)}, u32[]{:S(2)}, u32[]{:S(2)}) async-start(bf16[32,16,512]{2,1,0:T(8,128)(2,1)} %bitcast.6), calls=%async_computation | async-start | bytes 1048576 | tf_op jit(solution)/shard_map/all_to_all | solution.py:406
  59.9 12.7 %collective-permute-start.8 = (bf16[288,256]{1,0:T(8,128)(2,1)}, bf16[288,256]{1,0:T(8,128)(2,1)S(1)}, u32[]{:S(2)}, u32[]{:S(2)}) collective-permute-start(bf16[288,256]{1,0:T(8,128)(2,1)} %copy-done.10), channel_id=1, source_target_pairs={{0,224},{16,48},{32,0},{48,80},{64,32},{80,112},{96,64},{112,144},... | collective-permute-start | bytes 442376 | tf_op jit(solution)/shard_map/ppermute | solution.py:386
  65.8 6.4 %collective-permute-start.11 = (bf16[256,256]{1,0:T(8,128)(2,1)}, bf16[256,256]{1,0:T(8,128)(2,1)S(1)}, u32[]{:S(2)}, u32[]{:S(2)}) collective-permute-start(bf16[256,256]{1,0:T(8,128)(2,1)} %copy-done.11), channel_id=1, source_target_pairs={{0,32},{16,240},{32,64},{48,16},{64,96},{80,48},{96,128},{112,80},... | collective-permute-start | bytes 393224 | tf_op jit(solution)/shard_map/ppermute | solution.py:386
  72.3 10.0 %collective-permute-start.12 = (bf16[544,256]{1,0:T(8,128)(2,1)S(1)}, bf16[544,256]{1,0:T(8,128)(2,1)S(1)}, u32[]{:S(2)}, u32[]{:S(2)}) collective-permute-start(bf16[544,256]{1,0:T(8,128)(2,1)S(1)} %shard_map.111), channel_id=1, source_target_pairs={{0,32},{16,240},{32,64},{48,16},{64,96},{80,48},{96,128},{112,80},... | collective-permute-start | bytes 835592 | tf_op jit(solution)/shard_map/ppermute | solution.py:386
  72.7 9.8 %collective-permute-start.9 = (bf16[544,256]{1,0:T(8,128)(2,1)S(1)}, bf16[544,256]{1,0:T(8,128)(2,1)S(1)}, u32[]{:S(2)}, u32[]{:S(2)}) collective-permute-start(bf16[544,256]{1,0:T(8,128)(2,1)S(1)} %shard_map.108), channel_id=1, source_target_pairs={{0,224},{16,48},{32,0},{48,80},{64,32},{80,112},{96,64},{112,144},... | collective-permute-start | bytes 835592 | tf_op jit(solution)/shard_map/ppermute | solution.py:386
  82.4 11.5 %collective-permute-start.13 = (bf16[544,256]{1,0:T(8,128)(2,1)S(1)}, bf16[544,256]{1,0:T(8,128)(2,1)S(1)}, u32[]{:S(2)}, u32[]{:S(2)}) collective-permute-start(bf16[544,256]{1,0:T(8,128)(2,1)S(1)} %shard_map.112), channel_id=1, source_target_pairs={{0,32},{16,240},{32,64},{48,16},{64,96},{80,48},{96,128},{112,80},... | collective-permute-start | bytes 835592 | tf_op jit(solution)/shard_map/ppermute | solution.py:386
  82.6 11.4 %collective-permute-start.10 = (bf16[544,256]{1,0:T(8,128)(2,1)S(1)}, bf16[544,256]{1,0:T(8,128)(2,1)S(1)}, u32[]{:S(2)}, u32[]{:S(2)}) collective-permute-start(bf16[544,256]{1,0:T(8,128)(2,1)S(1)} %shard_map.109), channel_id=1, source_target_pairs={{0,224},{16,48},{32,0},{48,80},{64,32},{80,112},{96,64},{112,144},... | collective-permute-start | bytes 835592 | tf_op jit(solution)/shard_map/ppermute | solution.py:386
  86.6 14.3 %all-to-all-start.1 = ((bf16[16,16,512]{2,1,0:T(8,128)(2,1)}), bf16[16,16,512]{2,1,0:T(8,128)(2,1)S(1)}, u32[]{:S(2)}, u32[]{:S(2)}) async-start(bf16[16,16,512]{2,1,0:T(8,128)(2,1)} %shard_map.114), calls=%async_computation.1 | async-start | bytes 524288 | tf_op jit(solution)/shard_map/all_to_all | solution.py:408
  100.9 6.5 %collective-permute-start.14 = (bf16[544,256]{1,0:T(8,128)(2,1)S(1)}, bf16[544,256]{1,0:T(8,128)(2,1)S(1)}, u32[]{:S(2)}, u32[]{:S(2)}) collective-permute-start(bf16[544,256]{1,0:T(8,128)(2,1)S(1)} %shard_map.110), channel_id=1, source_target_pairs={{0,224},{16,48},{32,0},{48,80},{64,32},{80,112},{96,64},{112,144},... | collective-permute-start | bytes 835592 | tf_op jit(solution)/shard_map/ppermute | solution.py:386
  100.9 7.8 %collective-permute-start.15 = (bf16[544,256]{1,0:T(8,128)(2,1)S(1)}, bf16[544,256]{1,0:T(8,128)(2,1)S(1)}, u32[]{:S(2)}, u32[]{:S(2)}) collective-permute-start(bf16[544,256]{1,0:T(8,128)(2,1)S(1)} %shard_map.113), channel_id=1, source_target_pairs={{0,32},{16,240},{32,64},{48,16},{64,96},{80,48},{96,128},{112,80},... | collective-permute-start | bytes 835592 | tf_op jit(solution)/shard_map/ppermute | solution.py:386
  108.7 2.2 %copy-start.2 = (bf16[256,8192]{1,0:T(8,128)(2,1)S(1)}, bf16[256,8192]{1,0:T(8,128)(2,1)}, u32[]{:S(2)}) copy-start(bf16[256,8192]{1,0:T(8,128)(2,1)} %p_ref.5) | copy-start | bytes 12582916

commit v2 on v1

--- a/solution.py
+++ b/solution.py
@@ -64,7 +64,7 @@
     return values / length, length
 
 
-def prep_kernel(count_ref, index_ref, s_ref, t_ref, out_ref):
+def prep_kernel(count_ref, index_ref, s_ref, t_ref, out_ref, info_ref):
     for i in range(LOCAL):
         pick = picks(index_ref, count_ref[i], i)
         for which, ref in enumerate((s_ref, t_ref)):
@@ -74,8 +74,11 @@
     counts = jnp.zeros((HELD - ROWS, D), jnp.int32)
     for i in range(LOCAL):
         counts = jnp.where(row == i, count_ref[i], counts)
+    counts = counts.astype(f32)
     for which in range(2):
-        out_ref[which, ROWS:, :] = counts.astype(f32).astype(bf16)
+        out_ref[which, ROWS:, :] = counts.astype(bf16)
+    info_ref[:LOCAL, :] = counts[:LOCAL, :SLOTS]
+    info_ref[LOCAL:, :] = index_ref[...].astype(f32)
 
 
 def prep(count, index, student, teacher):
@@ -83,9 +86,9 @@
     vmem = pl.BlockSpec(memory_space=pltpu.VMEM)
     return pl.pallas_call(
         prep_kernel,
-        out_shape=jax.ShapeDtypeStruct((2, HELD, D), bf16),
+        out_shape=[jax.ShapeDtypeStruct((2, HELD, D), bf16), jax.ShapeDtypeStruct((2 * LOCAL, SLOTS), f32)],
         in_specs=[smem, vmem, vmem, vmem],
-        out_specs=vmem,
+        out_specs=[vmem, vmem],
         compiler_params=params(),
         cost_estimate=cost(2 * 2 * ROWS * D * D, 1 << 21),
     )(count, index, student, teacher)
@@ -358,9 +361,12 @@
     )(near, a, b, misc, prototypes)
 
 
-def final_kernel(count_ref, index_ref, s_ref, du_ref, out_ref):
+def final_kernel(info_ref, s_ref, du_ref, out_ref):
     for i in range(LOCAL):
-        pick = picks(index_ref, count_ref[i], i)
+        patch = lax.broadcasted_iota(jnp.int32, (D, SLOTS), 0).astype(f32)
+        slot = lax.broadcasted_iota(jnp.int32, (D, SLOTS), 1).astype(f32)
+        hit = (patch == info_ref[LOCAL + i : LOCAL + i + 1, :]) & (slot < info_ref[i : i + 1, :])
+        pick = jnp.where(hit, 1.0, 0.0).astype(bf16)
         unit, length = unit_rows(dot(pick, s_ref[i], TN))
         d_unit = du_ref[:, i * SLOTS : (i + 1) * SLOTS].astype(f32).T
         row = (d_unit - unit * jnp.sum(unit * d_unit, axis=1, keepdims=True)) / length
@@ -385,7 +391,7 @@
     def ring(value, pairs):
         return lax.ppermute(value, ("z", "core"), pairs)
 
-    mine = prep(mask_count, mask_index, student_rows, teacher_rows)
+    mine, info = prep(mask_count, mask_index, student_rows, teacher_rows)
     other = lax.ppermute(mine, "core", [(0, 1), (1, 0)])
     center = center.reshape(1, -1)
     stats, row_sum = local_stats(ids, prototypes, center, mine, other)
@@ -405,7 +411,6 @@
     part = D // (X * Y)
     got = lax.all_to_all(send.reshape(PEERS, part, ROWS), peers, 0, 0)
     own = small_call(du_sum_kernel, jax.ShapeDtypeStruct((X * Y, part, ROWS), bf16), got)
-    du = lax.all_to_all(own, ("x", "y"), 0, 0)
     for i in range(3):
         if i == 0:
             kernel_a = functools.partial(halves_kernel, 0, True)
@@ -415,14 +420,14 @@
         send_a = small_call(kernel_a, step_shape, near[2 * i], got_a, misc)
         send_b = small_call(kernel_b, step_shape, near[2 * i + 1], got_b, misc)
         if i == 2:
-            send_a, send_b, du = lax.optimization_barrier((send_a, send_b, du))
+            send_a, send_b, own = lax.optimization_barrier((send_a, send_b, own))
+            du = lax.all_to_all(own, ("x", "y"), 0, 0)
         got_a, got_b = ring(send_a, one_way), ring(send_b, other_way)
     proto_grad, patch_center, loss = finish(near[6], got_a, got_b, misc, prototypes)
     student_grad = small_call(
         final_kernel,
         jax.ShapeDtypeStruct(student_rows.shape, f32),
-        mask_count, mask_index, student_rows, du.reshape(D, ROWS),
-        smem=(0,),
+        info, student_rows, du.reshape(D, ROWS),
     )
     return (loss.reshape(()), student_grad, proto_grad, patch_center.reshape(-1))
 

time: 113 us -> 107 us (0.947); the launches traced: 113 us -> 105 us
  blocking collectives: 0 us -> 14.1 us
  waiting for transfers between devices: 31.4 us -> 22 us
  starting transfers between devices: 38.1 us -> 30.7 us
  local copies, waits for them, and re-layouts: 12.1 us -> 8.55 us
  Pallas kernels: 29.5 us -> 28.3 us
    all_to_all x0 -> x1, blocking collectives: none -> 14.1 us  [shards(): du = lax.all_to_all(own, ('x', 'y'), 0, 0)]
    ppermute x8, waiting for transfers between devices: 15.6 us -> 6.19 us  [ring(): return lax.ppermute(value, ('z', 'core'), pairs)]
    all_to_all x1 -> x0, starting transfers between devices: 7.27 us -> none  [shards(): du = lax.all_to_all(own, ('x', 'y'), 0, 0)]
    all_to_all x1, waiting for transfers between devices: 0.01 us -> 6.87 us  [shards(): got = lax.all_to_all(send.reshape(PEERS, part, ROWS), peers, 0, 0)]
    all_to_all x1 -> x0, waiting for transfers between devices: 6.82 us -> none  [shards(): du = lax.all_to_all(own, ('x', 'y'), 0, 0)]
    unnamed x28 -> x20, local copies, waits for them, and re-layouts: 12.1 us -> 8.55 us
    pallas_call x11, Pallas kernels: 4.68 us -> 3.42 us  [small_call(): pl.pallas_call(kernel, out_shape=out_shape, in_specs=specs, out_specs=jax...]
  transfers between devices with their start and end apart: 18 -> 17, of which waited for: 11 -> 8; matrix products, arithmetic and copies ran while one was open for 0% -> 0% of each run, Pallas kernels for 4% -> 3%
where the time goes in v2:
time: 107 us; the launch traced here: 105 us
  starting transfers between devices  30.7 us (29%)
  Pallas kernels  28.3 us (26%)
  waiting for transfers between devices  22 us (21%)
  blocking collectives  14.1 us (13%)
  local copies, waits for them, and re-layouts  8.55 us (8%)
  between operations  1.67 us (2%)
    ppermute x8, starting transfers between devices, ring(): return lax.ppermute(value, ('z', 'core'), pairs)  15 us
    all_to_all x1, blocking collectives, shards(): du = lax.all_to_all(own, ('x', 'y'), 0, 0)  14.1 us
    pallas_call x1, Pallas kernels, local_stats(): pl.pallas_call(stats_kernel, in_specs=[smem, vmem, vmem, vmem, vmem], out...  11.2 us
    pallas_call x1, Pallas kernels, grads(): pl.pallas_call(grad_kernel, in_specs=[smem] + [vmem] * 6, out_specs=[vmem...  10.9 us
    unnamed x20, local copies, waits for them, and re-layouts  8.55 us
    ppermute x6, starting transfers between devices, swaps(): lax.ppermute(value, axis, [(i, i ^ k) for i in range(4)])  8.52 us
    all_to_all x1, waiting for transfers between devices, shards(): got = lax.all_to_all(send.reshape(PEERS, part, ROWS), peers, 0, 0)  6.87 us
    all_to_all x1, starting transfers between devices, shards(): got = lax.all_to_all(send.reshape(PEERS, part, ROWS), peers, 0, 0)  6.73 us
  transfers between devices with their start and end apart: 17, of which 8 were waited for; matrix products, arithmetic and copies ran while one was open for 0% of the time, Pallas kernels for 3%

profile of v2, /device:TPU:8, one launch (start us, length us, event | category | flops | bytes accessed | tf_op | source)
XLA Modules:
  0.0 105.4 jit_solution(5332746170690634759)
XLA Ops:
  0.6 0.0 copy-start.3
  0.6 1.0 copy-done.3
  1.7 0.0 copy-start.5
  1.7 1.0 copy-done.5
  2.7 0.7 copy-done.6
  3.4 0.0 copy-start.7
  3.4 0.7 copy-done.7
  4.1 1.1 %shard_map.102 = (bf16[2,528,256]{2,1,0:T(8,128)(2,1)S(1)}, f32[8,128]{1,0:T(8,128)S(1)}) custom-call(s32[4]{0:T(128)S(1)} %copy-done.7, s32[4,128]{1,0:T(4,128)S(1)} %copy-done.6, bf16[4,256,256]{2,1,0:T(8,128)(2,1)S(1)} %copy-done.3, bf16[4,256,256]{2,1,0:T(8,128)(2,1)S(1)} %copy-done.5), custom_call_target="tpu_custom_call" | custom-call | flops 134217728 | bytes 2097152 | tf_op jit(solution)/shard_map/pallas_call | solution.py:87
  5.2 0.1 collective-permute-start
  5.3 0.1 pad_add_fusion.ids_ref
  5.3 1.8 %collective-permute-done.other_ref = bf16[2,528,256]{2,1,0:T(8,128)(2,1)S(1)} collective-permute-done((bf16[2,528,256]{2,1,0:T(8,128)(2,1)S(1)}, bf16[2,528,256]{2,1,0:T(8,128)(2,1)S(1)}, u32[]{:S(2)}, u32[]{:S(2)}) %collective-permute-start) | collective-permute-done | bytes 540704 | tf_op jit(solution)/shard_map/ppermute | solution.py:395
  7.2 0.0 copy-start
  7.2 2.2 %copy-done = bf16[256,8192]{1,0:T(8,128)(2,1)S(1)} copy-done((bf16[256,8192]{1,0:T(8,128)(2,1)S(1)}, bf16[256,8192]{1,0:T(8,128)(2,1)}, u32[]{:S(2)}) %copy-start) | copy-done | bytes 4194328
  9.4 0.0 copy-start.8
  9.4 0.8 copy-done.8
  10.1 0.0 copy-start.9
  10.1 11.2 %shard_map.103 = (f32[40,128]{1,0:T(8,128)S(1)}, f32[8,256]{1,0:T(8,128)S(1)}) custom-call(s32[4]{0:T(128)S(1)} %pad_add_fusion.ids_ref, bf16[256,8192]{1,0:T(8,128)(2,1)S(1)} %copy-done, f32[1,8192]{1,0:T(1,128)S(1)} %bitcast.12, bf16[2,528,256]{2,1,0:T(8,128)(2,1)S(1)} %get-tuple-element.26.mine_ref, bf16[2,528,256]{2,1,0:T(8,128)(2,1)S(1)} %collective-permute-done.other_ref), custom_call_target="tpu_custom_call" | custom-call | flops 4294967296 | bytes 6291456 | tf_op jit(solution)/shard_map/pallas_call | solution.py:154
  21.3 0.4 collective-permute-start.1
  21.7 1.1 collective-permute-done.1.got_ref
  22.8 1.7 %collective-permute-start.4 = (f32[40,128]{1,0:T(8,128)S(1)}, f32[40,128]{1,0:T(8,128)S(1)}, u32[]{:S(2)}, u32[]{:S(2)}) collective-permute-start(f32[40,128]{1,0:T(8,128)S(1)} %shard_map.104.a), channel_id=1, source_target_pairs={{0,3},{1,2},{2,1},{3,0},{4,7},{5,6},{6,5},{7,4},{8,11},{9,10},{10,... | collective-permute-start | bytes 61448 | tf_op jit(solution)/shard_map/ppermute | solution.py:389
  24.4 2.7 %collective-permute-start.3 = (f32[40,128]{1,0:T(8,128)S(1)}, f32[40,128]{1,0:T(8,128)S(1)}, u32[]{:S(2)}, u32[]{:S(2)}) collective-permute-start(f32[40,128]{1,0:T(8,128)S(1)} %shard_map.104.a), channel_id=1, source_target_pairs={{0,2},{1,3},{2,0},{3,1},{4,6},{5,7},{6,4},{7,5},{8,10},{9,11},{10,... | collective-permute-start | bytes 61448 | tf_op jit(solution)/shard_map/ppermute | solution.py:389
  27.1 0.0 collective-permute-start.2
  27.1 0.0 collective-permute-done.4.d
  27.1 2.7 %collective-permute-done.3.c = f32[40,128]{1,0:T(8,128)S(1)} collective-permute-done((f32[40,128]{1,0:T(8,128)S(1)}, f32[40,128]{1,0:T(8,128)S(1)}, u32[]{:S(2)}, u32[]{:S(2)}) %collective-permute-start.3) | collective-permute-done | bytes 20512 | tf_op jit(solution)/shard_map/ppermute | solution.py:389
  29.9 1.0 collective-permute-done.2.b
  30.9 1.8 %collective-permute-start.7 = (f32[40,128]{1,0:T(8,128)S(1)}, f32[40,128]{1,0:T(8,128)S(1)}, u32[]{:S(2)}, u32[]{:S(2)}) collective-permute-start(f32[40,128]{1,0:T(8,128)S(1)} %shard_map.105.a), channel_id=1, source_target_pairs={{0,12},{4,8},{8,4},{12,0},{1,13},{5,9},{9,5},{13,1},{2,14},{6,10},... | collective-permute-start | bytes 61448 | tf_op jit(solution)/shard_map/ppermute | solution.py:389
  32.8 0.8 collective-permute-start.6
  33.6 1.6 %collective-permute-start.5 = (f32[40,128]{1,0:T(8,128)S(1)}, f32[40,128]{1,0:T(8,128)S(1)}, u32[]{:S(2)}, u32[]{:S(2)}) collective-permute-start(f32[40,128]{1,0:T(8,128)S(1)} %shard_map.105.a), channel_id=1, source_target_pairs={{0,4},{4,0},{8,12},{12,8},{1,5},{5,1},{9,13},{13,9},{2,6},{6,2},{1... | collective-permute-start | bytes 61448 | tf_op jit(solution)/shard_map/ppermute | solution.py:389
  35.8 0.2 collective-permute-done.7.d
  36.0 2.0 %collective-permute-done.6.c = f32[40,128]{1,0:T(8,128)S(1)} collective-permute-done((f32[40,128]{1,0:T(8,128)S(1)}, f32[40,128]{1,0:T(8,128)S(1)}, u32[]{:S(2)}, u32[]{:S(2)}) %collective-permute-start.6) | collective-permute-done | bytes 20512 | tf_op jit(solution)/shard_map/ppermute | solution.py:389
  38.0 0.0 collective-permute-done.5.b
  38.0 0.7 shard_map.106
  38.7 0.0 copy-done.9
  38.7 0.0 copy-start.1
  38.7 2.2 %copy-done.1 = bf16[256,8192]{1,0:T(8,128)(2,1)S(1)} copy-done((bf16[256,8192]{1,0:T(8,128)(2,1)S(1)}, bf16[256,8192]{1,0:T(8,128)(2,1)}, u32[]{:S(2)}) %copy-start.1) | copy-done | bytes 4194328
  40.9 10.9 %shard_map.107 = (bf16[288,256]{1,0:T(8,128)(2,1)S(1)}, bf16[256,256]{1,0:T(8,128)(2,1)S(1)}, bf16[512,256]{1,0:T(8,128)(2,1)S(1)}, bf16[512,256]{1,0:T(8,128)(2...) custom-call(s32[4]{0:T(128)S(1)} %pad_add_fusion.ids_ref, ...), custom_call_target="tpu_custom_call" | custom-call | flops 8589934592 | bytes 8388608 | tf_op jit(solution)/shard_map/pallas_call | solution.py:295
  51.8 5.9 %collective-permute-start.8 = (bf16[288,256]{1,0:T(8,128)(2,1)S(1)}, bf16[288,256]{1,0:T(8,128)(2,1)S(1)}, u32[]{:S(2)}, u32[]{:S(2)}) collective-permute-start(bf16[288,256]{1,0:T(8,128)(2,1)S(1)} %get-tuple-element.35), channel_id=1, source_target_pairs={{0,224},{16,48},{32,0},{48,80},{64,32},{80,112},{96,64},{112,144},... | collective-permute-start | bytes 442376 | tf_op jit(solution)/shard_map/ppermute | solution.py:392
  57.7 0.0 collective-permute-start.11
  57.7 6.2 %collective-permute-done.11.got_ref = bf16[256,256]{1,0:T(8,128)(2,1)S(1)} collective-permute-done((bf16[256,256]{1,0:T(8,128)(2,1)S(1)}, bf16[256,256]{1,0:T(8,128)(2,1)S(1)}, u32[]{:S(2)}, u32[]{:S(2)}) %collective-permute-start.11) | collective-permute-done | bytes 131104 | tf_op jit(solution)/shard_map/ppermute | solution.py:392
  63.9 0.1 collective-permute-start.12
  64.0 0.0 collective-permute-done.8.got_ref
  64.0 3.5 %collective-permute-start.9 = (bf16[544,256]{1,0:T(8,128)(2,1)S(1)}, bf16[544,256]{1,0:T(8,128)(2,1)S(1)}, u32[]{:S(2)}, u32[]{:S(2)}) collective-permute-start(bf16[544,256]{1,0:T(8,128)(2,1)S(1)} %shard_map.108), channel_id=1, source_target_pairs={{0,224},{16,48},{32,0},{48,80},{64,32},{80,112},{96,64},{112,144},... | collective-permute-start | bytes 835592 | tf_op jit(solution)/shard_map/ppermute | solution.py:392
  67.6 6.7 %all-to-all-start = ((bf16[32,16,512]{2,1,0:T(8,128)(2,1)}), bf16[32,16,512]{2,1,0:T(8,128)(2,1)S(1)}, u32[]{:S(2)}, u32[]{:S(2)}) async-start(bf16[32,16,512]{2,1,0:T(8,128)(2,1)} %bitcast.6), calls=%async_computation | async-start | bytes 1048576 | tf_op jit(solution)/shard_map/all_to_all | solution.py:412
  74.3 0.0 collective-permute-done.12.got_ref
  74.3 0.1 shard_map.112
  74.4 0.1 collective-permute-start.13
  74.5 0.0 collective-permute-done.9.got_ref
  74.5 0.1 shard_map.109
  74.6 3.3 %collective-permute-start.10 = (bf16[544,256]{1,0:T(8,128)(2,1)S(1)}, bf16[544,256]{1,0:T(8,128)(2,1)S(1)}, u32[]{:S(2)}, u32[]{:S(2)}) collective-permute-start(bf16[544,256]{1,0:T(8,128)(2,1)S(1)} %shard_map.109), channel_id=1, source_target_pairs={{0,224},{16,48},{32,0},{48,80},{64,32},{80,112},{96,64},{112,144},... | collective-permute-start | bytes 835592 | tf_op jit(solution)/shard_map/ppermute | solution.py:392
  77.9 6.9 %all-to-all-done.got_ref = bf16[32,16,512]{2,1,0:T(8,128)(2,1)S(1)} async-done(((bf16[32,16,512]{2,1,0:T(8,128)(2,1)}), bf16[32,16,512]{2,1,0:T(8,128)(2,1)S(1)}, u32[]{:S(2)}, u32[]{:S(2)}) %all-to-all-start) | async-done | bytes 524320 | tf_op jit(solution)/shard_map/all_to_all | solution.py:412
  84.7 0.1 shard_map.114
  84.8 0.0 collective-permute-done.13.got_ref
  84.8 0.1 shard_map.113
  84.9 0.0 collective-permute-done.10.got_ref
  84.9 0.1 shard_map.110
  85.0 0.8 collective-permute-start.14
  85.8 1.3 %collective-permute-start.15 = (bf16[544,256]{1,0:T(8,128)(2,1)S(1)}, bf16[544,256]{1,0:T(8,128)(2,1)S(1)}, u32[]{:S(2)}, u32[]{:S(2)}) collective-permute-start(bf16[544,256]{1,0:T(8,128)(2,1)S(1)} %shard_map.113), channel_id=1, source_target_pairs={{0,32},{16,240},{32,64},{48,16},{64,96},{80,48},{96,128},{112,80},... | collective-permute-start | bytes 835592 | tf_op jit(solution)/shard_map/ppermute | solution.py:392
  87.1 14.1 %all_to_all.10 = bf16[16,16,512]{2,1,0:T(8,128)(2,1)S(1)} all-to-all(bf16[16,16,512]{2,1,0:T(8,128)(2,1)S(1)} %shard_map.114), channel_id=1, replica_groups=mesh['z'=8,'core'=2,'x'=4,'y'=4] {'x','y'}, dimensions={0} | all-to-all | bytes 524288 | tf_op jit(solution)/shard_map/all_to_all | solution.py:424
  101.2 0.0 copy-done.4
  101.2 2.3 %shard_map.116 = f32[4,256,256]{2,1,0:T(8,128)} custom-call(f32[8,128]{1,0:T(8,128)S(1)} %get-tuple-element.44.info_ref, bf16[4,256,256]{2,1,0:T(8,128)(2,1)S(1)} %copy-done.4, bf16[256,512]{1,0:T(8,128)(2,1)S(1)} %bitcast.11), custom_call_target="tpu_custom_call" | custom-call | flops 1048576 | bytes 262144 | tf_op jit(solution)/shard_map/pallas_call | solution.py:243
  103.5 0.0 collective-permute-done.14.a_ref
  103.5 0.0 collective-permute-done.15.b_ref
  103.5 0.0 copy-done.2
  103.5 1.7 %shard_map.115 = (f32[512,256]{1,0:T(8,128)}, f32[1,8192]{1,0:T(1,128)}, f32[1,1]{1,0:T(1,128)}) custom-call(bf16[512,256]{1,0:T(8,128)(2,1)S(1)} %get-tuple-element.31.near_ref, bf16[544,256]{1,0:T(8,128)(2,1)S(1)} %collective-permute-done.14.a_ref, bf16[544,256]{1,0:T(8,128)(2,1)S(1)} %collective-permute-done.15.b_ref, ...), custom_call_target="tpu_custom_call" | custom-call | flops 100663296 | bytes 5242880 | tf_op jit(solution)/shard_map/pallas_call | solution.py:350
  (7 shorter events, 0.1 us)
Async XLA Ops:
  0.6 1.0 copy-start.3
  1.7 1.0 copy-start.5
  2.7 0.7 copy-start.6
  3.4 0.7 copy-start.7
  5.2 2.0 %collective-permute-start = (bf16[2,528,256]{2,1,0:T(8,128)(2,1)S(1)}, bf16[2,528,256]{2,1,0:T(8,128)(2,1)S(1)}, u32[]{:S(2)}, u32[]{:S(2)}) collective-permute-start(bf16[2,528,256]{2,1,0:T(8,128)(2,1)S(1)} %get-tuple-element.26.mine_ref), channel_id=1, source_target_pairs={{0,16},{16,0},{1,17},{17,1},{2,18},{18,2},{3,19},{19,3},{4,20},{20... | collective-permute-start | bytes 1622024 | tf_op jit(solution)/shard_map/ppermute | solution.py:395
  7.2 2.2 %copy-start = (bf16[256,8192]{1,0:T(8,128)(2,1)S(1)}, bf16[256,8192]{1,0:T(8,128)(2,1)}, u32[]{:S(2)}) copy-start(bf16[256,8192]{1,0:T(8,128)(2,1)} %p_ref.5) | copy-start | bytes 12582916
  9.4 0.8 copy-start.8
  10.1 28.6 %copy-start.9 = (f32[8192]{0:T(1024)S(1)}, f32[8192]{0:T(1024)}, u32[]{:S(2)}) copy-start(f32[8192]{0:T(1024)} %param.10) | copy-start | bytes 98308
  21.3 1.5 %collective-permute-start.1 = (f32[40,128]{1,0:T(8,128)S(1)}, f32[40,128]{1,0:T(8,128)S(1)}, u32[]{:S(2)}, u32[]{:S(2)}) collective-permute-start(f32[40,128]{1,0:T(8,128)S(1)} %get-tuple-element.27.mine_ref), channel_id=1, source_target_pairs={{0,16},{16,0},{1,17},{17,1},{2,18},{18,2},{3,19},{19,3},{4,20},{20... | collective-permute-start | bytes 61448 | tf_op jit(solution)/shard_map/ppermute | solution.py:399
  22.8 4.3 %collective-permute-start.4 = (f32[40,128]{1,0:T(8,128)S(1)}, f32[40,128]{1,0:T(8,128)S(1)}, u32[]{:S(2)}, u32[]{:S(2)}) collective-permute-start(f32[40,128]{1,0:T(8,128)S(1)} %shard_map.104.a), channel_id=1, source_target_pairs={{0,3},{1,2},{2,1},{3,0},{4,7},{5,6},{6,5},{7,4},{8,11},{9,10},{10,... | collective-permute-start | bytes 61448 | tf_op jit(solution)/shard_map/ppermute | solution.py:389
  24.4 5.4 %collective-permute-start.3 = (f32[40,128]{1,0:T(8,128)S(1)}, f32[40,128]{1,0:T(8,128)S(1)}, u32[]{:S(2)}, u32[]{:S(2)}) collective-permute-start(f32[40,128]{1,0:T(8,128)S(1)} %shard_map.104.a), channel_id=1, source_target_pairs={{0,2},{1,3},{2,0},{3,1},{4,6},{5,7},{6,4},{7,5},{8,10},{9,11},{10,... | collective-permute-start | bytes 61448 | tf_op jit(solution)/shard_map/ppermute | solution.py:389
  27.1 3.8 %collective-permute-start.2 = (f32[40,128]{1,0:T(8,128)S(1)}, f32[40,128]{1,0:T(8,128)S(1)}, u32[]{:S(2)}, u32[]{:S(2)}) collective-permute-start(f32[40,128]{1,0:T(8,128)S(1)} %shard_map.104.a), channel_id=1, source_target_pairs={{0,1},{1,0},{2,3},{3,2},{4,5},{5,4},{6,7},{7,6},{8,9},{9,8},{10,11... | collective-permute-start | bytes 61448 | tf_op jit(solution)/shard_map/ppermute | solution.py:389
  30.9 5.1 %collective-permute-start.7 = (f32[40,128]{1,0:T(8,128)S(1)}, f32[40,128]{1,0:T(8,128)S(1)}, u32[]{:S(2)}, u32[]{:S(2)}) collective-permute-start(f32[40,128]{1,0:T(8,128)S(1)} %shard_map.105.a), channel_id=1, source_target_pairs={{0,12},{4,8},{8,4},{12,0},{1,13},{5,9},{9,5},{13,1},{2,14},{6,10},... | collective-permute-start | bytes 61448 | tf_op jit(solution)/shard_map/ppermute | solution.py:389
  32.8 5.3 %collective-permute-start.6 = (f32[40,128]{1,0:T(8,128)S(1)}, f32[40,128]{1,0:T(8,128)S(1)}, u32[]{:S(2)}, u32[]{:S(2)}) collective-permute-start(f32[40,128]{1,0:T(8,128)S(1)} %shard_map.105.a), channel_id=1, source_target_pairs={{0,8},{4,12},{8,0},{12,4},{1,9},{5,13},{9,1},{13,5},{2,10},{6,14},... | collective-permute-start | bytes 61448 | tf_op jit(solution)/shard_map/ppermute | solution.py:389
  33.6 4.5 %collective-permute-start.5 = (f32[40,128]{1,0:T(8,128)S(1)}, f32[40,128]{1,0:T(8,128)S(1)}, u32[]{:S(2)}, u32[]{:S(2)}) collective-permute-start(f32[40,128]{1,0:T(8,128)S(1)} %shard_map.105.a), channel_id=1, source_target_pairs={{0,4},{4,0},{8,12},{12,8},{1,5},{5,1},{9,13},{13,9},{2,6},{6,2},{1... | collective-permute-start | bytes 61448 | tf_op jit(solution)/shard_map/ppermute | solution.py:389
  38.7 2.2 %copy-start.1 = (bf16[256,8192]{1,0:T(8,128)(2,1)S(1)}, bf16[256,8192]{1,0:T(8,128)(2,1)}, u32[]{:S(2)}) copy-start(bf16[256,8192]{1,0:T(8,128)(2,1)} %p_ref.5) | copy-start | bytes 12582916
  51.8 49.4 %copy-start.4 = (bf16[4,256,256]{2,1,0:T(8,128)(2,1)S(1)}, bf16[4,256,256]{2,1,0:T(8,128)(2,1)}, u32[]{:S(2)}) copy-start(bf16[4,256,256]{2,1,0:T(8,128)(2,1)} %s_ref.3) | copy-start | bytes 1572868
  51.8 12.2 %collective-permute-start.8 = (bf16[288,256]{1,0:T(8,128)(2,1)S(1)}, bf16[288,256]{1,0:T(8,128)(2,1)S(1)}, u32[]{:S(2)}, u32[]{:S(2)}) collective-permute-start(bf16[288,256]{1,0:T(8,128)(2,1)S(1)} %get-tuple-element.35), channel_id=1, source_target_pairs={{0,224},{16,48},{32,0},{48,80},{64,32},{80,112},{96,64},{112,144},... | collective-permute-start | bytes 442376 | tf_op jit(solution)/shard_map/ppermute | solution.py:392
  57.7 6.2 %collective-permute-start.11 = (bf16[256,256]{1,0:T(8,128)(2,1)S(1)}, bf16[256,256]{1,0:T(8,128)(2,1)S(1)}, u32[]{:S(2)}, u32[]{:S(2)}) collective-permute-start(bf16[256,256]{1,0:T(8,128)(2,1)S(1)} %get-tuple-element.39), channel_id=1, source_target_pairs={{0,32},{16,240},{32,64},{48,16},{64,96},{80,48},{96,128},{112,80},... | collective-permute-start | bytes 393224 | tf_op jit(solution)/shard_map/ppermute | solution.py:392
  63.9 10.4 %collective-permute-start.12 = (bf16[544,256]{1,0:T(8,128)(2,1)S(1)}, bf16[544,256]{1,0:T(8,128)(2,1)S(1)}, u32[]{:S(2)}, u32[]{:S(2)}) collective-permute-start(bf16[544,256]{1,0:T(8,128)(2,1)S(1)} %shard_map.111), channel_id=1, source_target_pairs={{0,32},{16,240},{32,64},{48,16},{64,96},{80,48},{96,128},{112,80},... | collective-permute-start | bytes 835592 | tf_op jit(solution)/shard_map/ppermute | solution.py:392
  64.0 10.5 %collective-permute-start.9 = (bf16[544,256]{1,0:T(8,128)(2,1)S(1)}, bf16[544,256]{1,0:T(8,128)(2,1)S(1)}, u32[]{:S(2)}, u32[]{:S(2)}) collective-permute-start(bf16[544,256]{1,0:T(8,128)(2,1)S(1)} %shard_map.108), channel_id=1, source_target_pairs={{0,224},{16,48},{32,0},{48,80},{64,32},{80,112},{96,64},{112,144},... | collective-permute-start | bytes 835592 | tf_op jit(solution)/shard_map/ppermute | solution.py:392
  67.6 17.2 %all-to-all-start = ((bf16[32,16,512]{2,1,0:T(8,128)(2,1)}), bf16[32,16,512]{2,1,0:T(8,128)(2,1)S(1)}, u32[]{:S(2)}, u32[]{:S(2)}) async-start(bf16[32,16,512]{2,1,0:T(8,128)(2,1)} %bitcast.6), calls=%async_computation | async-start | bytes 1048576 | tf_op jit(solution)/shard_map/all_to_all | solution.py:412
  74.4 10.4 %collective-permute-start.13 = (bf16[544,256]{1,0:T(8,128)(2,1)S(1)}, bf16[544,256]{1,0:T(8,128)(2,1)S(1)}, u32[]{:S(2)}, u32[]{:S(2)}) collective-permute-start(bf16[544,256]{1,0:T(8,128)(2,1)S(1)} %shard_map.112), channel_id=1, source_target_pairs={{0,32},{16,240},{32,64},{48,16},{64,96},{80,48},{96,128},{112,80},... | collective-permute-start | bytes 835592 | tf_op jit(solution)/shard_map/ppermute | solution.py:392
  74.6 10.3 %collective-permute-start.10 = (bf16[544,256]{1,0:T(8,128)(2,1)S(1)}, bf16[544,256]{1,0:T(8,128)(2,1)S(1)}, u32[]{:S(2)}, u32[]{:S(2)}) collective-permute-start(bf16[544,256]{1,0:T(8,128)(2,1)S(1)} %shard_map.109), channel_id=1, source_target_pairs={{0,224},{16,48},{32,0},{48,80},{64,32},{80,112},{96,64},{112,144},... | collective-permute-start | bytes 835592 | tf_op jit(solution)/shard_map/ppermute | solution.py:392
  84.7 18.8 %copy-start.2 = (bf16[256,8192]{1,0:T(8,128)(2,1)S(1)}, bf16[256,8192]{1,0:T(8,128)(2,1)}, u32[]{:S(2)}) copy-start(bf16[256,8192]{1,0:T(8,128)(2,1)} %p_ref.5) | copy-start | bytes 12582916
  85.0 18.5 %collective-permute-start.14 = (bf16[544,256]{1,0:T(8,128)(2,1)S(1)}, bf16[544,256]{1,0:T(8,128)(2,1)S(1)}, u32[]{:S(2)}, u32[]{:S(2)}) collective-permute-start(bf16[544,256]{1,0:T(8,128)(2,1)S(1)} %shard_map.110), channel_id=1, source_target_pairs={{0,224},{16,48},{32,0},{48,80},{64,32},{80,112},{96,64},{112,144},... | collective-permute-start | bytes 835592 | tf_op jit(solution)/shard_map/ppermute | solution.py:392
  85.8 17.7 %collective-permute-start.15 = (bf16[544,256]{1,0:T(8,128)(2,1)S(1)}, bf16[544,256]{1,0:T(8,128)(2,1)S(1)}, u32[]{:S(2)}, u32[]{:S(2)}) collective-permute-start(bf16[544,256]{1,0:T(8,128)(2,1)S(1)} %shard_map.113), channel_id=1, source_target_pairs={{0,32},{16,240},{32,64},{48,16},{64,96},{80,48},{96,128},{112,80},... | collective-permute-start | bytes 835592 | tf_op jit(solution)/shard_map/ppermute | solution.py:392

commit v3 on v2

--- a/solution.py
+++ b/solution.py
@@ -98,8 +98,8 @@
     return jnp.concatenate([block] * times, axis=1)
 
 
-def chunk_columns(i, core):
-    return pl.ds(pl.multiple_of((CORES * i + core) * CHUNK, CHUNK), CHUNK)
+def chunk_columns(i):
+    return pl.ds(i * CHUNK, CHUNK) if isinstance(i, int) else pl.ds(pl.multiple_of(i * CHUNK, CHUNK), CHUNK)
 
 
 def turned(held):
@@ -109,7 +109,7 @@
 def stats_kernel(ids_ref, p_ref, c_ref, mine_ref, other_ref, block, sum_ref, acc):
     groups = (CHUNK // 8, 8, STAT_TILE)
     for i in range(Z):
-        columns = chunk_columns(i, ids_ref[1])
+        columns = chunk_columns(i)
         protos = p_ref[:, columns].T
         shift = wide(turned(c_ref[:, columns]), STAT_TILE // 128)
         for half, ref in enumerate((mine_ref, other_ref)):
@@ -256,7 +256,7 @@
     core = ids_ref[1]
     order = [lax.rem(ids_ref[0] + Z + d * (1 - 2 * core), Z) for d in OFFSETS]
     for i in range(n):
-        columns = chunk_columns(order[i], core)
+        columns = chunk_columns(order[i])
         wide_p = p_ref[:, columns]
         protos = wide_p.T
         shift = wide(turned(c_ref[:, columns]), TILE // 128)
@@ -394,7 +394,10 @@
     mine, info = prep(mask_count, mask_index, student_rows, teacher_rows)
     other = lax.ppermute(mine, "core", [(0, 1), (1, 0)])
     center = center.reshape(1, -1)
-    stats, row_sum = local_stats(ids, prototypes, center, mine, other)
+    here = [(CORES * i + core) * CHUNK for i in range(Z)]
+    half = jnp.concatenate([lax.dynamic_slice(prototypes, (0, at), (D, CHUNK)) for at in here], axis=1)
+    center = jnp.concatenate([lax.dynamic_slice(center, (0, at), (1, CHUNK)) for at in here], axis=1)
+    stats, row_sum = local_stats(ids, half, center, mine, other)
     shape = jax.ShapeDtypeStruct((STATS * 8, 128), f32)
     stats = small_call(core_merge_kernel, shape, stats, lax.ppermute(stats, "core", [(0, 1), (1, 0)]))
     stats = small_call(y_merge_kernel, shape, stats, *swaps(stats, "y"))
@@ -406,7 +409,7 @@
     )
 
     step_shape = jax.ShapeDtypeStruct((CHUNK + EXTRA, D), bf16)
-    half_a, half_b, *near, send = grads(ids, prototypes, center, mine, other, coef, misc)
+    half_a, half_b, *near, send = grads(ids, half, center, mine, other, coef, misc)
     got_a, got_b = ring(half_a, one_way), ring(half_b, other_way)
     part = D // (X * Y)
     got = lax.all_to_all(send.reshape(PEERS, part, ROWS), peers, 0, 0)

time: 107 us -> 110 us (1.028)
  local copies, waits for them, and re-layouts: 8.55 us -> 13.8 us
  waiting for transfers between devices: 22 us -> 19.9 us
    unnamed x20 -> x30, local copies, waits for them, and re-layouts: 8.55 us -> 11.9 us
    ppermute x1, waiting for transfers between devices: 1.84 us -> 0.01 us  [shards(): other = lax.ppermute(mine, 'core', [(0, 1), (1, 0)])]
  transfers between devices with their start and end apart: 17 -> 17, of which waited for: 8 -> 7; matrix products, arithmetic and copies ran while one was open for 0% -> 8% of each run, Pallas kernels for 3% -> 2%
where the time goes in v3:
time: 110 us; the launch traced here: 109 us
  starting transfers between devices  30.9 us (28%)
  Pallas kernels  28.2 us (26%)
  waiting for transfers between devices  19.9 us (18%)
  blocking collectives  14.1 us (13%)
  local copies, waits for them, and re-layouts  13.8 us (13%)
  between operations  1.78 us (2%)
    ppermute x8, starting transfers between devices, ring(): return lax.ppermute(value, ('z', 'core'), pairs)  14.7 us
    all_to_all x1, blocking collectives, shards(): du = lax.all_to_all(own, ('x', 'y'), 0, 0)  14.1 us
    unnamed x30, local copies, waits for them, and re-layouts  11.9 us
    pallas_call x1, Pallas kernels, local_stats(): pl.pallas_call(stats_kernel, in_specs=[smem, vmem, vmem, vmem, vmem], out...  11.1 us
    pallas_call x1, Pallas kernels, grads(): pl.pallas_call(grad_kernel, in_specs=[smem] + [vmem] * 6, out_specs=[vmem...  10.9 us
    ppermute x6, starting transfers between devices, swaps(): lax.ppermute(value, axis, [(i, i ^ k) for i in range(4)])  8.52 us
    all_to_all x1, starting transfers between devices, shards(): got = lax.all_to_all(send.reshape(PEERS, part, ROWS), peers, 0, 0)  7.01 us
    all_to_all x1, waiting for transfers between devices, shards(): got = lax.all_to_all(send.reshape(PEERS, part, ROWS), peers, 0, 0)  6.86 us
  transfers between devices with their start and end apart: 17, of which 7 were waited for; matrix products, arithmetic and copies ran while one was open for 8% of the time, Pallas kernels for 2%

profile of v3, /device:TPU:8, one launch (start us, length us, event | category | flops | bytes accessed | tf_op | source)
XLA Modules:
  0.0 108.7 jit_solution(5859028943347112844)
XLA Ops:
  0.6 0.0 copy-start.1
  0.6 1.0 copy-done.1
  1.7 1.0 copy-done.3
  2.7 0.7 copy-done.6
  3.4 0.7 copy-done.7
  4.1 1.1 %shard_map.102 = (bf16[2,528,256]{2,1,0:T(8,128)(2,1)S(1)}, f32[8,128]{1,0:T(8,128)S(1)}) custom-call(s32[4]{0:T(128)S(1)} %copy-done.7, s32[4,128]{1,0:T(4,128)S(1)} %copy-done.6, bf16[4,256,256]{2,1,0:T(8,128)(2,1)S(1)} %copy-done.1, bf16[4,256,256]{2,1,0:T(8,128)(2,1)S(1)} %copy-done.3), custom_call_target="tpu_custom_call" | custom-call | flops 134217728 | bytes 2097152 | tf_op jit(solution)/shard_map/pallas_call | solution.py:87
  5.2 0.1 collective-permute-start
  5.3 0.9 fusion
  6.2 1.0 dynamic-slice_dynamic-update-slice_fusion.7
  7.2 1.0 dynamic-slice_dynamic-update-slice_fusion.6
  8.2 1.0 dynamic-slice_dynamic-update-slice_fusion.5
  9.1 1.0 dynamic-slice_dynamic-update-slice_fusion.4
  10.2 0.1 pad_add_fusion.ids_ref
  10.3 1.0 dynamic-slice_dynamic-update-slice_fusion.3
  11.3 1.0 dynamic-slice_dynamic-update-slice_fusion.2
  12.3 1.0 dynamic-slice_dynamic-update-slice_fusion.1
  13.3 1.0 dynamic-slice_dynamic-update-slice_fusion.p_ref
  14.3 0.0 collective-permute-done.other_ref
  14.3 11.1 %shard_map.103 = (f32[40,128]{1,0:T(8,128)S(1)}, f32[8,256]{1,0:T(8,128)S(1)}) custom-call(s32[4]{0:T(128)S(1)} %pad_add_fusion.ids_ref, bf16[256,4096]{1,0:T(8,128)(2,1)S(1)} %dynamic-slice_dynamic-update-slice_fusion.p_ref, f32[1,4096]{1,0:T(1,128)S(1)} %constant_dynamic-update-slice_fusion.c_ref, bf16[2,528,256]{2,1,0:T(8,128)(2,1)S(1)} %get-tuple-element.26.mine_ref, ...), custom_call_target="tpu_custom_call" | custom-call | flops 4294967296 | bytes 6291456 | tf_op jit(solution)/shard_map/pallas_call | solution.py:154
  25.4 0.5 collective-permute-start.1
  25.9 0.8 collective-permute-done.1.got_ref
  26.8 1.7 %collective-permute-start.4 = (f32[40,128]{1,0:T(8,128)S(1)}, f32[40,128]{1,0:T(8,128)S(1)}, u32[]{:S(2)}, u32[]{:S(2)}) collective-permute-start(f32[40,128]{1,0:T(8,128)S(1)} %shard_map.104.a), channel_id=1, source_target_pairs={{0,3},{1,2},{2,1},{3,0},{4,7},{5,6},{6,5},{7,4},{8,11},{9,10},{10,... | collective-permute-start | bytes 61448 | tf_op jit(solution)/shard_map/ppermute | solution.py:389
  28.4 2.7 %collective-permute-start.3 = (f32[40,128]{1,0:T(8,128)S(1)}, f32[40,128]{1,0:T(8,128)S(1)}, u32[]{:S(2)}, u32[]{:S(2)}) collective-permute-start(f32[40,128]{1,0:T(8,128)S(1)} %shard_map.104.a), channel_id=1, source_target_pairs={{0,2},{1,3},{2,0},{3,1},{4,6},{5,7},{6,4},{7,5},{8,10},{9,11},{10,... | collective-permute-start | bytes 61448 | tf_op jit(solution)/shard_map/ppermute | solution.py:389
  31.1 0.0 collective-permute-start.2
  31.1 0.0 collective-permute-done.4.d
  31.1 2.7 %collective-permute-done.3.c = f32[40,128]{1,0:T(8,128)S(1)} collective-permute-done((f32[40,128]{1,0:T(8,128)S(1)}, f32[40,128]{1,0:T(8,128)S(1)}, u32[]{:S(2)}, u32[]{:S(2)}) %collective-permute-start.3) | collective-permute-done | bytes 20512 | tf_op jit(solution)/shard_map/ppermute | solution.py:389
  33.8 1.1 collective-permute-done.2.b
  34.9 1.8 %collective-permute-start.7 = (f32[40,128]{1,0:T(8,128)S(1)}, f32[40,128]{1,0:T(8,128)S(1)}, u32[]{:S(2)}, u32[]{:S(2)}) collective-permute-start(f32[40,128]{1,0:T(8,128)S(1)} %shard_map.105.a), channel_id=1, source_target_pairs={{0,12},{4,8},{8,4},{12,0},{1,13},{5,9},{9,5},{13,1},{2,14},{6,10},... | collective-permute-start | bytes 61448 | tf_op jit(solution)/shard_map/ppermute | solution.py:389
  36.7 0.8 collective-permute-start.6
  37.5 1.6 %collective-permute-start.5 = (f32[40,128]{1,0:T(8,128)S(1)}, f32[40,128]{1,0:T(8,128)S(1)}, u32[]{:S(2)}, u32[]{:S(2)}) collective-permute-start(f32[40,128]{1,0:T(8,128)S(1)} %shard_map.105.a), channel_id=1, source_target_pairs={{0,4},{4,0},{8,12},{12,8},{1,5},{5,1},{9,13},{13,9},{2,6},{6,2},{1... | collective-permute-start | bytes 61448 | tf_op jit(solution)/shard_map/ppermute | solution.py:389
  39.8 0.2 collective-permute-done.7.d
  40.0 2.0 %collective-permute-done.6.c = f32[40,128]{1,0:T(8,128)S(1)} collective-permute-done((f32[40,128]{1,0:T(8,128)S(1)}, f32[40,128]{1,0:T(8,128)S(1)}, u32[]{:S(2)}, u32[]{:S(2)}) %collective-permute-start.6) | collective-permute-done | bytes 20512 | tf_op jit(solution)/shard_map/ppermute | solution.py:389
  42.0 0.0 collective-permute-done.5.b
  42.0 0.7 shard_map.106
  42.7 1.6 %copy-done.5 = bf16[256,4096]{1,0:T(8,128)(2,1)S(1)} copy-done((bf16[256,4096]{1,0:T(8,128)(2,1)S(1)}, bf16[256,4096]{1,0:T(8,128)(2,1)}, u32[]{:S(2)}) %copy-start.5) | copy-done | bytes 2097176
  44.3 10.9 %shard_map.107 = (bf16[288,256]{1,0:T(8,128)(2,1)S(1)}, bf16[256,256]{1,0:T(8,128)(2,1)S(1)}, bf16[512,256]{1,0:T(8,128)(2,1)S(1)}, bf16[512,256]{1,0:T(8,128)(2...) custom-call(s32[4]{0:T(128)S(1)} %pad_add_fusion.ids_ref, ...), custom_call_target="tpu_custom_call" | custom-call | flops 8589934592 | bytes 8388608 | tf_op jit(solution)/shard_map/pallas_call | solution.py:295
  55.2 5.9 %collective-permute-start.8 = (bf16[288,256]{1,0:T(8,128)(2,1)S(1)}, bf16[288,256]{1,0:T(8,128)(2,1)S(1)}, u32[]{:S(2)}, u32[]{:S(2)}) collective-permute-start(bf16[288,256]{1,0:T(8,128)(2,1)S(1)} %get-tuple-element.35), channel_id=1, source_target_pairs={{0,224},{16,48},{32,0},{48,80},{64,32},{80,112},{96,64},{112,144},... | collective-permute-start | bytes 442376 | tf_op jit(solution)/shard_map/ppermute | solution.py:392
  61.0 0.0 collective-permute-start.11
  61.0 6.2 %collective-permute-done.11.got_ref = bf16[256,256]{1,0:T(8,128)(2,1)S(1)} collective-permute-done((bf16[256,256]{1,0:T(8,128)(2,1)S(1)}, bf16[256,256]{1,0:T(8,128)(2,1)S(1)}, u32[]{:S(2)}, u32[]{:S(2)}) %collective-permute-start.11) | collective-permute-done | bytes 131104 | tf_op jit(solution)/shard_map/ppermute | solution.py:392
  67.2 0.1 collective-permute-start.12
  67.3 0.0 collective-permute-done.8.got_ref
  67.4 3.3 %collective-permute-start.9 = (bf16[544,256]{1,0:T(8,128)(2,1)S(1)}, bf16[544,256]{1,0:T(8,128)(2,1)S(1)}, u32[]{:S(2)}, u32[]{:S(2)}) collective-permute-start(bf16[544,256]{1,0:T(8,128)(2,1)S(1)} %shard_map.108), channel_id=1, source_target_pairs={{0,224},{16,48},{32,0},{48,80},{64,32},{80,112},{96,64},{112,144},... | collective-permute-start | bytes 835592 | tf_op jit(solution)/shard_map/ppermute | solution.py:392
  70.7 7.0 %all-to-all-start = ((bf16[32,16,512]{2,1,0:T(8,128)(2,1)}), bf16[32,16,512]{2,1,0:T(8,128)(2,1)S(1)}, u32[]{:S(2)}, u32[]{:S(2)}) async-start(bf16[32,16,512]{2,1,0:T(8,128)(2,1)} %bitcast.13), calls=%async_computation | async-start | bytes 1048576 | tf_op jit(solution)/shard_map/all_to_all | solution.py:415
  77.7 0.0 collective-permute-done.12.got_ref
  77.7 0.1 shard_map.112
  77.8 0.0 copy-start.2
  77.8 0.1 collective-permute-start.13
  77.9 0.0 collective-permute-done.9.got_ref
  77.9 0.1 shard_map.109
  77.9 3.3 %collective-permute-start.10 = (bf16[544,256]{1,0:T(8,128)(2,1)S(1)}, bf16[544,256]{1,0:T(8,128)(2,1)S(1)}, u32[]{:S(2)}, u32[]{:S(2)}) collective-permute-start(bf16[544,256]{1,0:T(8,128)(2,1)S(1)} %shard_map.109), channel_id=1, source_target_pairs={{0,224},{16,48},{32,0},{48,80},{64,32},{80,112},{96,64},{112,144},... | collective-permute-start | bytes 835592 | tf_op jit(solution)/shard_map/ppermute | solution.py:392
  81.2 6.9 %all-to-all-done.got_ref = bf16[32,16,512]{2,1,0:T(8,128)(2,1)S(1)} async-done(((bf16[32,16,512]{2,1,0:T(8,128)(2,1)}), bf16[32,16,512]{2,1,0:T(8,128)(2,1)S(1)}, u32[]{:S(2)}, u32[]{:S(2)}) %all-to-all-start) | async-done | bytes 524320 | tf_op jit(solution)/shard_map/all_to_all | solution.py:415
  88.1 0.1 shard_map.114
  88.2 0.0 collective-permute-done.13.got_ref
  88.2 0.1 shard_map.113
  88.3 0.0 collective-permute-done.10.got_ref
  88.3 0.1 shard_map.110
  88.4 0.8 collective-permute-start.14
  89.1 1.3 %collective-permute-start.15 = (bf16[544,256]{1,0:T(8,128)(2,1)S(1)}, bf16[544,256]{1,0:T(8,128)(2,1)S(1)}, u32[]{:S(2)}, u32[]{:S(2)}) collective-permute-start(bf16[544,256]{1,0:T(8,128)(2,1)S(1)} %shard_map.113), channel_id=1, source_target_pairs={{0,32},{16,240},{32,64},{48,16},{64,96},{80,48},{96,128},{112,80},... | collective-permute-start | bytes 835592 | tf_op jit(solution)/shard_map/ppermute | solution.py:392
  90.5 14.1 %all_to_all.10 = bf16[16,16,512]{2,1,0:T(8,128)(2,1)S(1)} all-to-all(bf16[16,16,512]{2,1,0:T(8,128)(2,1)S(1)} %shard_map.114), channel_id=1, replica_groups=mesh['z'=8,'core'=2,'x'=4,'y'=4] {'x','y'}, dimensions={0} | all-to-all | bytes 524288 | tf_op jit(solution)/shard_map/all_to_all | solution.py:427
  104.6 0.0 copy-done.2
  104.6 2.3 %shard_map.116 = f32[4,256,256]{2,1,0:T(8,128)} custom-call(f32[8,128]{1,0:T(8,128)S(1)} %get-tuple-element.44.info_ref, bf16[4,256,256]{2,1,0:T(8,128)(2,1)S(1)} %copy-done.2, bf16[256,512]{1,0:T(8,128)(2,1)S(1)} %bitcast.18), custom_call_target="tpu_custom_call" | custom-call | flops 1048576 | bytes 262144 | tf_op jit(solution)/shard_map/pallas_call | solution.py:243
  106.9 0.0 collective-permute-done.14.a_ref
  106.9 0.0 collective-permute-done.15.b_ref
  106.9 1.7 %shard_map.115 = (f32[512,256]{1,0:T(8,128)}, f32[1,8192]{1,0:T(1,128)}, f32[1,1]{1,0:T(1,128)}) custom-call(bf16[512,256]{1,0:T(8,128)(2,1)S(1)} %get-tuple-element.31.near_ref, bf16[544,256]{1,0:T(8,128)(2,1)S(1)} %collective-permute-done.14.a_ref, bf16[544,256]{1,0:T(8,128)(2,1)S(1)} %collective-permute-done.15.b_ref, ...), custom_call_target="tpu_custom_call" | custom-call | flops 100663296 | bytes 5242880 | tf_op jit(solution)/shard_map/pallas_call | solution.py:350
  (20 shorter events, 0.2 us)
Async XLA Ops:
  0.6 1.0 copy-start.1
  1.7 1.0 copy-start.3
  2.7 0.7 copy-start.6
  3.4 0.7 copy-start.7
  5.2 9.1 %collective-permute-start = (bf16[2,528,256]{2,1,0:T(8,128)(2,1)S(1)}, bf16[2,528,256]{2,1,0:T(8,128)(2,1)S(1)}, u32[]{:S(2)}, u32[]{:S(2)}) collective-permute-start(bf16[2,528,256]{2,1,0:T(8,128)(2,1)S(1)} %get-tuple-element.26.mine_ref), channel_id=1, source_target_pairs={{0,16},{16,0},{1,17},{17,1},{2,18},{18,2},{3,19},{19,3},{4,20},{20... | collective-permute-start | bytes 1622024 | tf_op jit(solution)/shard_map/ppermute | solution.py:395
  14.2 11.1 %copy-start.4 = (bf16[256,4096]{1,0:T(8,128)(2,1)}, bf16[256,4096]{1,0:T(8,128)(2,1)S(1)}, u32[]{:S(2)}) copy-start(bf16[256,4096]{1,0:T(8,128)(2,1)S(1)} %dynamic-slice_dynamic-update-slice_fusion.p_ref) | copy-start | bytes 6291460
  25.4 1.4 %collective-permute-start.1 = (f32[40,128]{1,0:T(8,128)S(1)}, f32[40,128]{1,0:T(8,128)S(1)}, u32[]{:S(2)}, u32[]{:S(2)}) collective-permute-start(f32[40,128]{1,0:T(8,128)S(1)} %get-tuple-element.27.mine_ref), channel_id=1, source_target_pairs={{0,16},{16,0},{1,17},{17,1},{2,18},{18,2},{3,19},{19,3},{4,20},{20... | collective-permute-start | bytes 61448 | tf_op jit(solution)/shard_map/ppermute | solution.py:402
  26.8 4.3 %collective-permute-start.4 = (f32[40,128]{1,0:T(8,128)S(1)}, f32[40,128]{1,0:T(8,128)S(1)}, u32[]{:S(2)}, u32[]{:S(2)}) collective-permute-start(f32[40,128]{1,0:T(8,128)S(1)} %shard_map.104.a), channel_id=1, source_target_pairs={{0,3},{1,2},{2,1},{3,0},{4,7},{5,6},{6,5},{7,4},{8,11},{9,10},{10,... | collective-permute-start | bytes 61448 | tf_op jit(solution)/shard_map/ppermute | solution.py:389
  28.4 5.4 %collective-permute-start.3 = (f32[40,128]{1,0:T(8,128)S(1)}, f32[40,128]{1,0:T(8,128)S(1)}, u32[]{:S(2)}, u32[]{:S(2)}) collective-permute-start(f32[40,128]{1,0:T(8,128)S(1)} %shard_map.104.a), channel_id=1, source_target_pairs={{0,2},{1,3},{2,0},{3,1},{4,6},{5,7},{6,4},{7,5},{8,10},{9,11},{10,... | collective-permute-start | bytes 61448 | tf_op jit(solution)/shard_map/ppermute | solution.py:389
  31.1 3.8 %collective-permute-start.2 = (f32[40,128]{1,0:T(8,128)S(1)}, f32[40,128]{1,0:T(8,128)S(1)}, u32[]{:S(2)}, u32[]{:S(2)}) collective-permute-start(f32[40,128]{1,0:T(8,128)S(1)} %shard_map.104.a), channel_id=1, source_target_pairs={{0,1},{1,0},{2,3},{3,2},{4,5},{5,4},{6,7},{7,6},{8,9},{9,8},{10,11... | collective-permute-start | bytes 61448 | tf_op jit(solution)/shard_map/ppermute | solution.py:389
  34.9 5.1 %collective-permute-start.7 = (f32[40,128]{1,0:T(8,128)S(1)}, f32[40,128]{1,0:T(8,128)S(1)}, u32[]{:S(2)}, u32[]{:S(2)}) collective-permute-start(f32[40,128]{1,0:T(8,128)S(1)} %shard_map.105.a), channel_id=1, source_target_pairs={{0,12},{4,8},{8,4},{12,0},{1,13},{5,9},{9,5},{13,1},{2,14},{6,10},... | collective-permute-start | bytes 61448 | tf_op jit(solution)/shard_map/ppermute | solution.py:389
  36.7 5.3 %collective-permute-start.6 = (f32[40,128]{1,0:T(8,128)S(1)}, f32[40,128]{1,0:T(8,128)S(1)}, u32[]{:S(2)}, u32[]{:S(2)}) collective-permute-start(f32[40,128]{1,0:T(8,128)S(1)} %shard_map.105.a), channel_id=1, source_target_pairs={{0,8},{4,12},{8,0},{12,4},{1,9},{5,13},{9,1},{13,5},{2,10},{6,14},... | collective-permute-start | bytes 61448 | tf_op jit(solution)/shard_map/ppermute | solution.py:389
  37.5 4.5 %collective-permute-start.5 = (f32[40,128]{1,0:T(8,128)S(1)}, f32[40,128]{1,0:T(8,128)S(1)}, u32[]{:S(2)}, u32[]{:S(2)}) collective-permute-start(f32[40,128]{1,0:T(8,128)S(1)} %shard_map.105.a), channel_id=1, source_target_pairs={{0,4},{4,0},{8,12},{12,8},{1,5},{5,1},{9,13},{13,9},{2,6},{6,2},{1... | collective-permute-start | bytes 61448 | tf_op jit(solution)/shard_map/ppermute | solution.py:389
  42.7 1.6 %copy-start.5 = (bf16[256,4096]{1,0:T(8,128)(2,1)S(1)}, bf16[256,4096]{1,0:T(8,128)(2,1)}, u32[]{:S(2)}) copy-start(bf16[256,4096]{1,0:T(8,128)(2,1)} %copy-done.4) | copy-start | bytes 6291460
  55.2 12.2 %collective-permute-start.8 = (bf16[288,256]{1,0:T(8,128)(2,1)S(1)}, bf16[288,256]{1,0:T(8,128)(2,1)S(1)}, u32[]{:S(2)}, u32[]{:S(2)}) collective-permute-start(bf16[288,256]{1,0:T(8,128)(2,1)S(1)} %get-tuple-element.35), channel_id=1, source_target_pairs={{0,224},{16,48},{32,0},{48,80},{64,32},{80,112},{96,64},{112,144},... | collective-permute-start | bytes 442376 | tf_op jit(solution)/shard_map/ppermute | solution.py:392
  61.0 6.2 %collective-permute-start.11 = (bf16[256,256]{1,0:T(8,128)(2,1)S(1)}, bf16[256,256]{1,0:T(8,128)(2,1)S(1)}, u32[]{:S(2)}, u32[]{:S(2)}) collective-permute-start(bf16[256,256]{1,0:T(8,128)(2,1)S(1)} %get-tuple-element.39), channel_id=1, source_target_pairs={{0,32},{16,240},{32,64},{48,16},{64,96},{80,48},{96,128},{112,80},... | collective-permute-start | bytes 393224 | tf_op jit(solution)/shard_map/ppermute | solution.py:392
  67.2 10.4 %collective-permute-start.12 = (bf16[544,256]{1,0:T(8,128)(2,1)S(1)}, bf16[544,256]{1,0:T(8,128)(2,1)S(1)}, u32[]{:S(2)}, u32[]{:S(2)}) collective-permute-start(bf16[544,256]{1,0:T(8,128)(2,1)S(1)} %shard_map.111), channel_id=1, source_target_pairs={{0,32},{16,240},{32,64},{48,16},{64,96},{80,48},{96,128},{112,80},... | collective-permute-start | bytes 835592 | tf_op jit(solution)/shard_map/ppermute | solution.py:392
  67.4 10.5 %collective-permute-start.9 = (bf16[544,256]{1,0:T(8,128)(2,1)S(1)}, bf16[544,256]{1,0:T(8,128)(2,1)S(1)}, u32[]{:S(2)}, u32[]{:S(2)}) collective-permute-start(bf16[544,256]{1,0:T(8,128)(2,1)S(1)} %shard_map.108), channel_id=1, source_target_pairs={{0,224},{16,48},{32,0},{48,80},{64,32},{80,112},{96,64},{112,144},... | collective-permute-start | bytes 835592 | tf_op jit(solution)/shard_map/ppermute | solution.py:392
  70.7 17.4 %all-to-all-start = ((bf16[32,16,512]{2,1,0:T(8,128)(2,1)}), bf16[32,16,512]{2,1,0:T(8,128)(2,1)S(1)}, u32[]{:S(2)}, u32[]{:S(2)}) async-start(bf16[32,16,512]{2,1,0:T(8,128)(2,1)} %bitcast.13), calls=%async_computation | async-start | bytes 1048576 | tf_op jit(solution)/shard_map/all_to_all | solution.py:415
  77.8 26.8 %copy-start.2 = (bf16[4,256,256]{2,1,0:T(8,128)(2,1)S(1)}, bf16[4,256,256]{2,1,0:T(8,128)(2,1)}, u32[]{:S(2)}) copy-start(bf16[4,256,256]{2,1,0:T(8,128)(2,1)} %s_ref.3) | copy-start | bytes 1572868
  77.8 10.4 %collective-permute-start.13 = (bf16[544,256]{1,0:T(8,128)(2,1)S(1)}, bf16[544,256]{1,0:T(8,128)(2,1)S(1)}, u32[]{:S(2)}, u32[]{:S(2)}) collective-permute-start(bf16[544,256]{1,0:T(8,128)(2,1)S(1)} %shard_map.112), channel_id=1, source_target_pairs={{0,32},{16,240},{32,64},{48,16},{64,96},{80,48},{96,128},{112,80},... | collective-permute-start | bytes 835592 | tf_op jit(solution)/shard_map/ppermute | solution.py:392
  77.9 10.3 %collective-permute-start.10 = (bf16[544,256]{1,0:T(8,128)(2,1)S(1)}, bf16[544,256]{1,0:T(8,128)(2,1)S(1)}, u32[]{:S(2)}, u32[]{:S(2)}) collective-permute-start(bf16[544,256]{1,0:T(8,128)(2,1)S(1)} %shard_map.109), channel_id=1, source_target_pairs={{0,224},{16,48},{32,0},{48,80},{64,32},{80,112},{96,64},{112,144},... | collective-permute-start | bytes 835592 | tf_op jit(solution)/shard_map/ppermute | solution.py:392
  88.1 18.8 %copy-start = (bf16[256,8192]{1,0:T(8,128)(2,1)S(1)}, bf16[256,8192]{1,0:T(8,128)(2,1)}, u32[]{:S(2)}) copy-start(bf16[256,8192]{1,0:T(8,128)(2,1)} %p_ref.1) | copy-start | bytes 12582916
  88.4 18.5 %collective-permute-start.14 = (bf16[544,256]{1,0:T(8,128)(2,1)S(1)}, bf16[544,256]{1,0:T(8,128)(2,1)S(1)}, u32[]{:S(2)}, u32[]{:S(2)}) collective-permute-start(bf16[544,256]{1,0:T(8,128)(2,1)S(1)} %shard_map.110), channel_id=1, source_target_pairs={{0,224},{16,48},{32,0},{48,80},{64,32},{80,112},{96,64},{112,144},... | collective-permute-start | bytes 835592 | tf_op jit(solution)/shard_map/ppermute | solution.py:392
  89.1 17.7 %collective-permute-start.15 = (bf16[544,256]{1,0:T(8,128)(2,1)S(1)}, bf16[544,256]{1,0:T(8,128)(2,1)S(1)}, u32[]{:S(2)}, u32[]{:S(2)}) collective-permute-start(bf16[544,256]{1,0:T(8,128)(2,1)S(1)} %shard_map.113), channel_id=1, source_target_pairs={{0,32},{16,240},{32,64},{48,16},{64,96},{80,48},{96,128},{112,80},... | collective-permute-start | bytes 835592 | tf_op jit(solution)/shard_map/ppermute | solution.py:392

commit v4 on v2

--- a/solution.py
+++ b/solution.py
@@ -424,6 +424,7 @@
             du = lax.all_to_all(own, ("x", "y"), 0, 0)
         got_a, got_b = ring(send_a, one_way), ring(send_b, other_way)
     proto_grad, patch_center, loss = finish(near[6], got_a, got_b, misc, prototypes)
+    loss, du = lax.optimization_barrier((loss, du))
     student_grad = small_call(
         final_kernel,
         jax.ShapeDtypeStruct(student_rows.shape, f32),

time: 107 us -> 105 us (0.981)
  blocking collectives: 14.1 us -> 0 us
  starting transfers between devices: 30.7 us -> 37 us
  waiting for transfers between devices: 22 us -> 25.5 us
  local copies, waits for them, and re-layouts: 8.55 us -> 10.7 us
    all_to_all x1 -> x0, blocking collectives: 14.1 us -> none  [shards(): du = lax.all_to_all(own, ('x', 'y'), 0, 0)]
    all_to_all x0 -> x1, starting transfers between devices: none -> 6.29 us  [shards(): du = lax.all_to_all(own, ('x', 'y'), 0, 0)]
    unnamed x20, local copies, waits for them, and re-layouts: 8.55 us -> 10.7 us
    all_to_all x0 -> x1, waiting for transfers between devices: none -> 1.99 us  [shards(): du = lax.all_to_all(own, ('x', 'y'), 0, 0)]
    ppermute x8, waiting for transfers between devices: 6.19 us -> 7.67 us  [ring(): return lax.ppermute(value, ('z', 'core'), pairs)]
  transfers between devices with their start and end apart: 17 -> 18, of which waited for: 8 -> 11; matrix products, arithmetic and copies ran while one was open for 0% -> 0% of each run, Pallas kernels for 3% -> 3%
where the time goes in v4:
time: 105 us; the launch traced here: 104 us
  starting transfers between devices  37 us (35%)
  Pallas kernels  29 us (28%)
  waiting for transfers between devices  25.5 us (24%)
  local copies, waits for them, and re-layouts  10.7 us (10%)
  between operations  1.47 us (1%)
    ppermute x8, starting transfers between devices, ring(): return lax.ppermute(value, ('z', 'core'), pairs)  15 us
    pallas_call x1, Pallas kernels, local_stats(): pl.pallas_call(stats_kernel, in_specs=[smem, vmem, vmem, vmem, vmem], out...  11.2 us
    pallas_call x1, Pallas kernels, grads(): pl.pallas_call(grad_kernel, in_specs=[smem] + [vmem] * 6, out_specs=[vmem...  10.9 us
    unnamed x20, local copies, waits for them, and re-layouts  10.7 us
    ppermute x6, starting transfers between devices, swaps(): lax.ppermute(value, axis, [(i, i ^ k) for i in range(4)])  8.52 us
    ppermute x8, waiting for transfers between devices, ring(): return lax.ppermute(value, ('z', 'core'), pairs)  7.67 us
    all_to_all x1, waiting for transfers between devices, shards(): got = lax.all_to_all(send.reshape(PEERS, part, ROWS), peers, 0, 0)  6.86 us
    all_to_all x1, starting transfers between devices, shards(): got = lax.all_to_all(send.reshape(PEERS, part, ROWS), peers, 0, 0)  6.73 us
  transfers between devices with their start and end apart: 18, of which 11 were waited for; matrix products, arithmetic and copies ran while one was open for 0% of the time, Pallas kernels for 3%

profile of v4, /device:TPU:8, one launch (start us, length us, event | category | flops | bytes accessed | tf_op | source)
XLA Modules:
  0.0 103.7 jit_solution(10867629874447255191)
XLA Ops:
  0.6 0.0 copy-start.3
  0.6 1.0 copy-done.3
  1.7 0.0 copy-start.5
  1.7 1.0 %copy-done.5 = bf16[4,256,256]{2,1,0:T(8,128)(2,1)S(1)} copy-done((bf16[4,256,256]{2,1,0:T(8,128)(2,1)S(1)}, bf16[4,256,256]{2,1,0:T(8,128)(2,1)}, u32[]{:S(2)}) %copy-start.5) | copy-done | bytes 524312
  2.7 0.0 copy-start.6
  2.7 0.7 copy-done.6
  3.4 0.0 copy-start.7
  3.4 0.7 copy-done.7
  4.1 1.1 %shard_map.102 = (bf16[2,528,256]{2,1,0:T(8,128)(2,1)S(1)}, f32[8,128]{1,0:T(8,128)S(1)}) custom-call(s32[4]{0:T(128)S(1)} %copy-done.7, s32[4,128]{1,0:T(4,128)S(1)} %copy-done.6, bf16[4,256,256]{2,1,0:T(8,128)(2,1)S(1)} %copy-done.3, bf16[4,256,256]{2,1,0:T(8,128)(2,1)S(1)} %copy-done.5), custom_call_target="tpu_custom_call" | custom-call | flops 134217728 | bytes 2097152 | tf_op jit(solution)/shard_map/pallas_call | solution.py:87
  5.2 0.1 collective-permute-start
  5.3 0.1 pad_add_fusion.ids_ref
  5.3 1.8 %collective-permute-done.other_ref = bf16[2,528,256]{2,1,0:T(8,128)(2,1)S(1)} collective-permute-done((bf16[2,528,256]{2,1,0:T(8,128)(2,1)S(1)}, bf16[2,528,256]{2,1,0:T(8,128)(2,1)S(1)}, u32[]{:S(2)}, u32[]{:S(2)}) %collective-permute-start) | collective-permute-done | bytes 540704 | tf_op jit(solution)/shard_map/ppermute | solution.py:395
  7.2 2.2 %copy-done = bf16[256,8192]{1,0:T(8,128)(2,1)S(1)} copy-done((bf16[256,8192]{1,0:T(8,128)(2,1)S(1)}, bf16[256,8192]{1,0:T(8,128)(2,1)}, u32[]{:S(2)}) %copy-start) | copy-done | bytes 4194328
  9.4 0.8 copy-done.8
  10.1 11.2 %shard_map.103 = (f32[40,128]{1,0:T(8,128)S(1)}, f32[8,256]{1,0:T(8,128)S(1)}) custom-call(s32[4]{0:T(128)S(1)} %pad_add_fusion.ids_ref, bf16[256,8192]{1,0:T(8,128)(2,1)S(1)} %copy-done, f32[1,8192]{1,0:T(1,128)S(1)} %bitcast.12, bf16[2,528,256]{2,1,0:T(8,128)(2,1)S(1)} %get-tuple-element.28.mine_ref, bf16[2,528,256]{2,1,0:T(8,128)(2,1)S(1)} %collective-permute-done.other_ref), custom_call_target="tpu_custom_call" | custom-call | flops 4294967296 | bytes 6291456 | tf_op jit(solution)/shard_map/pallas_call | solution.py:154
  21.3 0.4 collective-permute-start.1
  21.7 1.1 %collective-permute-done.1.got_ref = f32[40,128]{1,0:T(8,128)S(1)} collective-permute-done((f32[40,128]{1,0:T(8,128)S(1)}, f32[40,128]{1,0:T(8,128)S(1)}, u32[]{:S(2)}, u32[]{:S(2)}) %collective-permute-start.1) | collective-permute-done | bytes 20512 | tf_op jit(solution)/shard_map/ppermute | solution.py:399
  22.8 1.7 %collective-permute-start.4 = (f32[40,128]{1,0:T(8,128)S(1)}, f32[40,128]{1,0:T(8,128)S(1)}, u32[]{:S(2)}, u32[]{:S(2)}) collective-permute-start(f32[40,128]{1,0:T(8,128)S(1)} %shard_map.104.a), channel_id=1, source_target_pairs={{0,3},{1,2},{2,1},{3,0},{4,7},{5,6},{6,5},{7,4},{8,11},{9,10},{10,... | collective-permute-start | bytes 61448 | tf_op jit(solution)/shard_map/ppermute | solution.py:389
  24.4 2.7 %collective-permute-start.3 = (f32[40,128]{1,0:T(8,128)S(1)}, f32[40,128]{1,0:T(8,128)S(1)}, u32[]{:S(2)}, u32[]{:S(2)}) collective-permute-start(f32[40,128]{1,0:T(8,128)S(1)} %shard_map.104.a), channel_id=1, source_target_pairs={{0,2},{1,3},{2,0},{3,1},{4,6},{5,7},{6,4},{7,5},{8,10},{9,11},{10,... | collective-permute-start | bytes 61448 | tf_op jit(solution)/shard_map/ppermute | solution.py:389
  27.1 0.0 collective-permute-start.2
  27.1 0.0 collective-permute-done.4.d
  27.1 2.7 %collective-permute-done.3.c = f32[40,128]{1,0:T(8,128)S(1)} collective-permute-done((f32[40,128]{1,0:T(8,128)S(1)}, f32[40,128]{1,0:T(8,128)S(1)}, u32[]{:S(2)}, u32[]{:S(2)}) %collective-permute-start.3) | collective-permute-done | bytes 20512 | tf_op jit(solution)/shard_map/ppermute | solution.py:389
  29.9 1.0 %collective-permute-done.2.b = f32[40,128]{1,0:T(8,128)S(1)} collective-permute-done((f32[40,128]{1,0:T(8,128)S(1)}, f32[40,128]{1,0:T(8,128)S(1)}, u32[]{:S(2)}, u32[]{:S(2)}) %collective-permute-start.2) | collective-permute-done | bytes 20512 | tf_op jit(solution)/shard_map/ppermute | solution.py:389
  30.9 1.8 %collective-permute-start.7 = (f32[40,128]{1,0:T(8,128)S(1)}, f32[40,128]{1,0:T(8,128)S(1)}, u32[]{:S(2)}, u32[]{:S(2)}) collective-permute-start(f32[40,128]{1,0:T(8,128)S(1)} %shard_map.105.a), channel_id=1, source_target_pairs={{0,12},{4,8},{8,4},{12,0},{1,13},{5,9},{9,5},{13,1},{2,14},{6,10},... | collective-permute-start | bytes 61448 | tf_op jit(solution)/shard_map/ppermute | solution.py:389
  32.8 0.8 collective-permute-start.6
  33.6 1.6 %collective-permute-start.5 = (f32[40,128]{1,0:T(8,128)S(1)}, f32[40,128]{1,0:T(8,128)S(1)}, u32[]{:S(2)}, u32[]{:S(2)}) collective-permute-start(f32[40,128]{1,0:T(8,128)S(1)} %shard_map.105.a), channel_id=1, source_target_pairs={{0,4},{4,0},{8,12},{12,8},{1,5},{5,1},{9,13},{13,9},{2,6},{6,2},{1... | collective-permute-start | bytes 61448 | tf_op jit(solution)/shard_map/ppermute | solution.py:389
  35.8 0.2 collective-permute-done.7.d
  36.0 2.0 %collective-permute-done.6.c = f32[40,128]{1,0:T(8,128)S(1)} collective-permute-done((f32[40,128]{1,0:T(8,128)S(1)}, f32[40,128]{1,0:T(8,128)S(1)}, u32[]{:S(2)}, u32[]{:S(2)}) %collective-permute-start.6) | collective-permute-done | bytes 20512 | tf_op jit(solution)/shard_map/ppermute | solution.py:389
  38.0 0.0 collective-permute-done.5.b
  38.0 0.7 shard_map.106
  38.7 0.0 copy-done.9
  38.7 0.0 copy-start.1
  38.7 2.2 %copy-done.1 = bf16[256,8192]{1,0:T(8,128)(2,1)S(1)} copy-done((bf16[256,8192]{1,0:T(8,128)(2,1)S(1)}, bf16[256,8192]{1,0:T(8,128)(2,1)}, u32[]{:S(2)}) %copy-start.1) | copy-done | bytes 4194328
  40.9 10.9 %shard_map.107 = (bf16[288,256]{1,0:T(8,128)(2,1)S(1)}, bf16[256,256]{1,0:T(8,128)(2,1)S(1)}, bf16[512,256]{1,0:T(8,128)(2,1)S(1)}, bf16[512,256]{1,0:T(8,128)(2...) custom-call(s32[4]{0:T(128)S(1)} %pad_add_fusion.ids_ref, ...), custom_call_target="tpu_custom_call" | custom-call | flops 8589934592 | bytes 8388608 | tf_op jit(solution)/shard_map/pallas_call | solution.py:295
  51.8 5.9 %collective-permute-start.8 = (bf16[288,256]{1,0:T(8,128)(2,1)S(1)}, bf16[288,256]{1,0:T(8,128)(2,1)S(1)}, u32[]{:S(2)}, u32[]{:S(2)}) collective-permute-start(bf16[288,256]{1,0:T(8,128)(2,1)S(1)} %get-tuple-element.37), channel_id=1, source_target_pairs={{0,224},{16,48},{32,0},{48,80},{64,32},{80,112},{96,64},{112,144},... | collective-permute-start | bytes 442376 | tf_op jit(solution)/shard_map/ppermute | solution.py:392
  57.7 0.0 collective-permute-start.11
  57.7 6.2 %collective-permute-done.11.got_ref = bf16[256,256]{1,0:T(8,128)(2,1)S(1)} collective-permute-done((bf16[256,256]{1,0:T(8,128)(2,1)S(1)}, bf16[256,256]{1,0:T(8,128)(2,1)S(1)}, u32[]{:S(2)}, u32[]{:S(2)}) %collective-permute-start.11) | collective-permute-done | bytes 131104 | tf_op jit(solution)/shard_map/ppermute | solution.py:392
  63.9 0.1 collective-permute-start.12
  64.0 0.0 collective-permute-done.8.got_ref
  64.0 3.5 %collective-permute-start.9 = (bf16[544,256]{1,0:T(8,128)(2,1)S(1)}, bf16[544,256]{1,0:T(8,128)(2,1)S(1)}, u32[]{:S(2)}, u32[]{:S(2)}) collective-permute-start(bf16[544,256]{1,0:T(8,128)(2,1)S(1)} %shard_map.108), channel_id=1, source_target_pairs={{0,224},{16,48},{32,0},{48,80},{64,32},{80,112},{96,64},{112,144},... | collective-permute-start | bytes 835592 | tf_op jit(solution)/shard_map/ppermute | solution.py:392
  67.6 6.7 %all-to-all-start = ((bf16[32,16,512]{2,1,0:T(8,128)(2,1)}), bf16[32,16,512]{2,1,0:T(8,128)(2,1)S(1)}, u32[]{:S(2)}, u32[]{:S(2)}) async-start(bf16[32,16,512]{2,1,0:T(8,128)(2,1)} %bitcast.6), calls=%async_computation | async-start | bytes 1048576 | tf_op jit(solution)/shard_map/all_to_all | solution.py:412
  74.3 0.0 collective-permute-done.12.got_ref
  74.3 0.1 shard_map.112
  74.4 0.1 collective-permute-start.13
  74.5 0.0 collective-permute-done.9.got_ref
  74.5 0.1 shard_map.109
  74.6 0.0 copy-start.4
  74.6 3.3 %collective-permute-start.10 = (bf16[544,256]{1,0:T(8,128)(2,1)S(1)}, bf16[544,256]{1,0:T(8,128)(2,1)S(1)}, u32[]{:S(2)}, u32[]{:S(2)}) collective-permute-start(bf16[544,256]{1,0:T(8,128)(2,1)S(1)} %shard_map.109), channel_id=1, source_target_pairs={{0,224},{16,48},{32,0},{48,80},{64,32},{80,112},{96,64},{112,144},... | collective-permute-start | bytes 835592 | tf_op jit(solution)/shard_map/ppermute | solution.py:392
  77.9 6.9 %all-to-all-done.got_ref = bf16[32,16,512]{2,1,0:T(8,128)(2,1)S(1)} async-done(((bf16[32,16,512]{2,1,0:T(8,128)(2,1)}), bf16[32,16,512]{2,1,0:T(8,128)(2,1)S(1)}, u32[]{:S(2)}, u32[]{:S(2)}) %all-to-all-start) | async-done | bytes 524320 | tf_op jit(solution)/shard_map/all_to_all | solution.py:412
  84.7 0.8 shard_map.114
  85.5 0.0 collective-permute-done.13.got_ref
  85.5 0.1 shard_map.113
  85.6 0.0 collective-permute-done.10.got_ref
  85.6 0.1 shard_map.110
  85.7 0.1 collective-permute-start.14
  85.8 2.0 %collective-permute-start.15 = (bf16[544,256]{1,0:T(8,128)(2,1)S(1)}, bf16[544,256]{1,0:T(8,128)(2,1)S(1)}, u32[]{:S(2)}, u32[]{:S(2)}) collective-permute-start(bf16[544,256]{1,0:T(8,128)(2,1)S(1)} %shard_map.113), channel_id=1, source_target_pairs={{0,32},{16,240},{32,64},{48,16},{64,96},{80,48},{96,128},{112,80},... | collective-permute-start | bytes 835592 | tf_op jit(solution)/shard_map/ppermute | solution.py:392
  87.8 6.3 %all-to-all-start.1 = ((bf16[16,16,512]{2,1,0:T(8,128)(2,1)}), bf16[16,16,512]{2,1,0:T(8,128)(2,1)S(1)}, u32[]{:S(2)}, u32[]{:S(2)}) async-start(bf16[16,16,512]{2,1,0:T(8,128)(2,1)} %shard_map.114), calls=%async_computation.1 | async-start | bytes 524288 | tf_op jit(solution)/shard_map/all_to_all | solution.py:424
  94.1 0.4 collective-permute-done.14.a_ref
  94.4 1.1 %collective-permute-done.15.b_ref = bf16[544,256]{1,0:T(8,128)(2,1)S(1)} collective-permute-done((bf16[544,256]{1,0:T(8,128)(2,1)S(1)}, bf16[544,256]{1,0:T(8,128)(2,1)S(1)}, u32[]{:S(2)}, u32[]{:S(2)}) %collective-permute-start.15) | collective-permute-done | bytes 278560 | tf_op jit(solution)/shard_map/ppermute | solution.py:392
  95.6 2.2 %copy-done.2 = bf16[256,8192]{1,0:T(8,128)(2,1)S(1)} copy-done((bf16[256,8192]{1,0:T(8,128)(2,1)S(1)}, bf16[256,8192]{1,0:T(8,128)(2,1)}, u32[]{:S(2)}) %copy-start.2) | copy-done | bytes 4194328
  97.8 1.7 %shard_map.115 = (f32[512,256]{1,0:T(8,128)}, f32[1,8192]{1,0:T(1,128)}, f32[1,1]{1,0:T(1,128)}) custom-call(bf16[512,256]{1,0:T(8,128)(2,1)S(1)} %get-tuple-element.33.near_ref, bf16[544,256]{1,0:T(8,128)(2,1)S(1)} %collective-permute-done.14.a_ref, bf16[544,256]{1,0:T(8,128)(2,1)S(1)} %collective-permute-done.15.b_ref, ...), custom_call_target="tpu_custom_call" | custom-call | flops 100663296 | bytes 5242880 | tf_op jit(solution)/shard_map/pallas_call | solution.py:350
  99.4 2.0 %all-to-all-done.1 = bf16[16,16,512]{2,1,0:T(8,128)(2,1)S(1)} async-done(((bf16[16,16,512]{2,1,0:T(8,128)(2,1)}), bf16[16,16,512]{2,1,0:T(8,128)(2,1)S(1)}, u32[]{:S(2)}, u32[]{:S(2)}) %all-to-all-start.1) | async-done | bytes 262176 | tf_op jit(solution)/shard_map/all_to_all | solution.py:424
  101.4 0.0 copy-done.4
  101.4 2.3 %shard_map.116 = f32[4,256,256]{2,1,0:T(8,128)} custom-call(f32[8,128]{1,0:T(8,128)S(1)} %get-tuple-element.48.info_ref, bf16[4,256,256]{2,1,0:T(8,128)(2,1)S(1)} %copy-done.4, bf16[256,512]{1,0:T(8,128)(2,1)S(1)} %bitcast.11), custom_call_target="tpu_custom_call" | custom-call | flops 1048576 | bytes 262144 | tf_op jit(solution)/shard_map/pallas_call | solution.py:243
  (8 shorter events, 0.1 us)
Async XLA Ops:
  0.6 1.0 %copy-start.3 = (bf16[4,256,256]{2,1,0:T(8,128)(2,1)S(1)}, bf16[4,256,256]{2,1,0:T(8,128)(2,1)}, u32[]{:S(2)}) copy-start(bf16[4,256,256]{2,1,0:T(8,128)(2,1)} %s_ref.3) | copy-start | bytes 1572868
  1.7 1.0 %copy-start.5 = (bf16[4,256,256]{2,1,0:T(8,128)(2,1)S(1)}, bf16[4,256,256]{2,1,0:T(8,128)(2,1)}, u32[]{:S(2)}) copy-start(bf16[4,256,256]{2,1,0:T(8,128)(2,1)} %t_ref.1) | copy-start | bytes 1572868
  2.7 0.7 copy-start.6
  3.4 0.7 copy-start.7
  5.2 2.0 %collective-permute-start = (bf16[2,528,256]{2,1,0:T(8,128)(2,1)S(1)}, bf16[2,528,256]{2,1,0:T(8,128)(2,1)S(1)}, u32[]{:S(2)}, u32[]{:S(2)}) collective-permute-start(bf16[2,528,256]{2,1,0:T(8,128)(2,1)S(1)} %get-tuple-element.28.mine_ref), channel_id=1, source_target_pairs={{0,16},{16,0},{1,17},{17,1},{2,18},{18,2},{3,19},{19,3},{4,20},{20... | collective-permute-start | bytes 1622024 | tf_op jit(solution)/shard_map/ppermute | solution.py:395
  7.2 2.2 %copy-start = (bf16[256,8192]{1,0:T(8,128)(2,1)S(1)}, bf16[256,8192]{1,0:T(8,128)(2,1)}, u32[]{:S(2)}) copy-start(bf16[256,8192]{1,0:T(8,128)(2,1)} %p_ref.5) | copy-start | bytes 12582916
  9.4 0.8 copy-start.8
  10.1 28.6 %copy-start.9 = (f32[8192]{0:T(1024)S(1)}, f32[8192]{0:T(1024)}, u32[]{:S(2)}) copy-start(f32[8192]{0:T(1024)} %param.10) | copy-start | bytes 98308
  21.3 1.5 %collective-permute-start.1 = (f32[40,128]{1,0:T(8,128)S(1)}, f32[40,128]{1,0:T(8,128)S(1)}, u32[]{:S(2)}, u32[]{:S(2)}) collective-permute-start(f32[40,128]{1,0:T(8,128)S(1)} %get-tuple-element.29.mine_ref), channel_id=1, source_target_pairs={{0,16},{16,0},{1,17},{17,1},{2,18},{18,2},{3,19},{19,3},{4,20},{20... | collective-permute-start | bytes 61448 | tf_op jit(solution)/shard_map/ppermute | solution.py:399
  22.8 4.3 %collective-permute-start.4 = (f32[40,128]{1,0:T(8,128)S(1)}, f32[40,128]{1,0:T(8,128)S(1)}, u32[]{:S(2)}, u32[]{:S(2)}) collective-permute-start(f32[40,128]{1,0:T(8,128)S(1)} %shard_map.104.a), channel_id=1, source_target_pairs={{0,3},{1,2},{2,1},{3,0},{4,7},{5,6},{6,5},{7,4},{8,11},{9,10},{10,... | collective-permute-start | bytes 61448 | tf_op jit(solution)/shard_map/ppermute | solution.py:389
  24.4 5.4 %collective-permute-start.3 = (f32[40,128]{1,0:T(8,128)S(1)}, f32[40,128]{1,0:T(8,128)S(1)}, u32[]{:S(2)}, u32[]{:S(2)}) collective-permute-start(f32[40,128]{1,0:T(8,128)S(1)} %shard_map.104.a), channel_id=1, source_target_pairs={{0,2},{1,3},{2,0},{3,1},{4,6},{5,7},{6,4},{7,5},{8,10},{9,11},{10,... | collective-permute-start | bytes 61448 | tf_op jit(solution)/shard_map/ppermute | solution.py:389
  27.1 3.8 %collective-permute-start.2 = (f32[40,128]{1,0:T(8,128)S(1)}, f32[40,128]{1,0:T(8,128)S(1)}, u32[]{:S(2)}, u32[]{:S(2)}) collective-permute-start(f32[40,128]{1,0:T(8,128)S(1)} %shard_map.104.a), channel_id=1, source_target_pairs={{0,1},{1,0},{2,3},{3,2},{4,5},{5,4},{6,7},{7,6},{8,9},{9,8},{10,11... | collective-permute-start | bytes 61448 | tf_op jit(solution)/shard_map/ppermute | solution.py:389
  30.9 5.1 %collective-permute-start.7 = (f32[40,128]{1,0:T(8,128)S(1)}, f32[40,128]{1,0:T(8,128)S(1)}, u32[]{:S(2)}, u32[]{:S(2)}) collective-permute-start(f32[40,128]{1,0:T(8,128)S(1)} %shard_map.105.a), channel_id=1, source_target_pairs={{0,12},{4,8},{8,4},{12,0},{1,13},{5,9},{9,5},{13,1},{2,14},{6,10},... | collective-permute-start | bytes 61448 | tf_op jit(solution)/shard_map/ppermute | solution.py:389
  32.8 5.3 %collective-permute-start.6 = (f32[40,128]{1,0:T(8,128)S(1)}, f32[40,128]{1,0:T(8,128)S(1)}, u32[]{:S(2)}, u32[]{:S(2)}) collective-permute-start(f32[40,128]{1,0:T(8,128)S(1)} %shard_map.105.a), channel_id=1, source_target_pairs={{0,8},{4,12},{8,0},{12,4},{1,9},{5,13},{9,1},{13,5},{2,10},{6,14},... | collective-permute-start | bytes 61448 | tf_op jit(solution)/shard_map/ppermute | solution.py:389
  33.6 4.5 %collective-permute-start.5 = (f32[40,128]{1,0:T(8,128)S(1)}, f32[40,128]{1,0:T(8,128)S(1)}, u32[]{:S(2)}, u32[]{:S(2)}) collective-permute-start(f32[40,128]{1,0:T(8,128)S(1)} %shard_map.105.a), channel_id=1, source_target_pairs={{0,4},{4,0},{8,12},{12,8},{1,5},{5,1},{9,13},{13,9},{2,6},{6,2},{1... | collective-permute-start | bytes 61448 | tf_op jit(solution)/shard_map/ppermute | solution.py:389
  38.7 2.2 %copy-start.1 = (bf16[256,8192]{1,0:T(8,128)(2,1)S(1)}, bf16[256,8192]{1,0:T(8,128)(2,1)}, u32[]{:S(2)}) copy-start(bf16[256,8192]{1,0:T(8,128)(2,1)} %p_ref.5) | copy-start | bytes 12582916
  51.8 12.2 %collective-permute-start.8 = (bf16[288,256]{1,0:T(8,128)(2,1)S(1)}, bf16[288,256]{1,0:T(8,128)(2,1)S(1)}, u32[]{:S(2)}, u32[]{:S(2)}) collective-permute-start(bf16[288,256]{1,0:T(8,128)(2,1)S(1)} %get-tuple-element.37), channel_id=1, source_target_pairs={{0,224},{16,48},{32,0},{48,80},{64,32},{80,112},{96,64},{112,144},... | collective-permute-start | bytes 442376 | tf_op jit(solution)/shard_map/ppermute | solution.py:392
  57.7 6.2 %collective-permute-start.11 = (bf16[256,256]{1,0:T(8,128)(2,1)S(1)}, bf16[256,256]{1,0:T(8,128)(2,1)S(1)}, u32[]{:S(2)}, u32[]{:S(2)}) collective-permute-start(bf16[256,256]{1,0:T(8,128)(2,1)S(1)} %get-tuple-element.41), channel_id=1, source_target_pairs={{0,32},{16,240},{32,64},{48,16},{64,96},{80,48},{96,128},{112,80},... | collective-permute-start | bytes 393224 | tf_op jit(solution)/shard_map/ppermute | solution.py:392
  63.9 10.4 %collective-permute-start.12 = (bf16[544,256]{1,0:T(8,128)(2,1)S(1)}, bf16[544,256]{1,0:T(8,128)(2,1)S(1)}, u32[]{:S(2)}, u32[]{:S(2)}) collective-permute-start(bf16[544,256]{1,0:T(8,128)(2,1)S(1)} %shard_map.111), channel_id=1, source_target_pairs={{0,32},{16,240},{32,64},{48,16},{64,96},{80,48},{96,128},{112,80},... | collective-permute-start | bytes 835592 | tf_op jit(solution)/shard_map/ppermute | solution.py:392
  64.0 10.5 %collective-permute-start.9 = (bf16[544,256]{1,0:T(8,128)(2,1)S(1)}, bf16[544,256]{1,0:T(8,128)(2,1)S(1)}, u32[]{:S(2)}, u32[]{:S(2)}) collective-permute-start(bf16[544,256]{1,0:T(8,128)(2,1)S(1)} %shard_map.108), channel_id=1, source_target_pairs={{0,224},{16,48},{32,0},{48,80},{64,32},{80,112},{96,64},{112,144},... | collective-permute-start | bytes 835592 | tf_op jit(solution)/shard_map/ppermute | solution.py:392
  67.6 17.2 %all-to-all-start = ((bf16[32,16,512]{2,1,0:T(8,128)(2,1)}), bf16[32,16,512]{2,1,0:T(8,128)(2,1)S(1)}, u32[]{:S(2)}, u32[]{:S(2)}) async-start(bf16[32,16,512]{2,1,0:T(8,128)(2,1)} %bitcast.6), calls=%async_computation | async-start | bytes 1048576 | tf_op jit(solution)/shard_map/all_to_all | solution.py:412
  74.4 11.1 %collective-permute-start.13 = (bf16[544,256]{1,0:T(8,128)(2,1)S(1)}, bf16[544,256]{1,0:T(8,128)(2,1)S(1)}, u32[]{:S(2)}, u32[]{:S(2)}) collective-permute-start(bf16[544,256]{1,0:T(8,128)(2,1)S(1)} %shard_map.112), channel_id=1, source_target_pairs={{0,32},{16,240},{32,64},{48,16},{64,96},{80,48},{96,128},{112,80},... | collective-permute-start | bytes 835592 | tf_op jit(solution)/shard_map/ppermute | solution.py:392
  74.6 26.8 %copy-start.4 = (bf16[4,256,256]{2,1,0:T(8,128)(2,1)S(1)}, bf16[4,256,256]{2,1,0:T(8,128)(2,1)}, u32[]{:S(2)}) copy-start(bf16[4,256,256]{2,1,0:T(8,128)(2,1)} %s_ref.3) | copy-start | bytes 1572868
  74.6 11.0 %collective-permute-start.10 = (bf16[544,256]{1,0:T(8,128)(2,1)S(1)}, bf16[544,256]{1,0:T(8,128)(2,1)S(1)}, u32[]{:S(2)}, u32[]{:S(2)}) collective-permute-start(bf16[544,256]{1,0:T(8,128)(2,1)S(1)} %shard_map.109), channel_id=1, source_target_pairs={{0,224},{16,48},{32,0},{48,80},{64,32},{80,112},{96,64},{112,144},... | collective-permute-start | bytes 835592 | tf_op jit(solution)/shard_map/ppermute | solution.py:392
  85.7 8.8 %collective-permute-start.14 = (bf16[544,256]{1,0:T(8,128)(2,1)S(1)}, bf16[544,256]{1,0:T(8,128)(2,1)S(1)}, u32[]{:S(2)}, u32[]{:S(2)}) collective-permute-start(bf16[544,256]{1,0:T(8,128)(2,1)S(1)} %shard_map.110), channel_id=1, source_target_pairs={{0,224},{16,48},{32,0},{48,80},{64,32},{80,112},{96,64},{112,144},... | collective-permute-start | bytes 835592 | tf_op jit(solution)/shard_map/ppermute | solution.py:392
  85.8 9.8 %collective-permute-start.15 = (bf16[544,256]{1,0:T(8,128)(2,1)S(1)}, bf16[544,256]{1,0:T(8,128)(2,1)S(1)}, u32[]{:S(2)}, u32[]{:S(2)}) collective-permute-start(bf16[544,256]{1,0:T(8,128)(2,1)S(1)} %shard_map.113), channel_id=1, source_target_pairs={{0,32},{16,240},{32,64},{48,16},{64,96},{80,48},{96,128},{112,80},... | collective-permute-start | bytes 835592 | tf_op jit(solution)/shard_map/ppermute | solution.py:392
  87.8 13.6 %all-to-all-start.1 = ((bf16[16,16,512]{2,1,0:T(8,128)(2,1)}), bf16[16,16,512]{2,1,0:T(8,128)(2,1)S(1)}, u32[]{:S(2)}, u32[]{:S(2)}) async-start(bf16[16,16,512]{2,1,0:T(8,128)(2,1)} %shard_map.114), calls=%async_computation.1 | async-start | bytes 524288 | tf_op jit(solution)/shard_map/all_to_all | solution.py:424
  95.6 2.2 %copy-start.2 = (bf16[256,8192]{1,0:T(8,128)(2,1)S(1)}, bf16[256,8192]{1,0:T(8,128)(2,1)}, u32[]{:S(2)}) copy-start(bf16[256,8192]{1,0:T(8,128)(2,1)} %p_ref.5) | copy-start | bytes 12582916
